TPU v7x, 32 devices: a whole 2x2x4 slice. The times are simulated.
32 devices in a mesh: dp: 16 (over z, y, x), tensor: 2 (over core).
Axes of the slice: x: 2, y: 2, z: 4, core: 2. Of those that a mesh axis runs over, the one named last changes fastest.
Arguments:
- frames: bfloat16 [16, 1536, 768], P('dp'), may hold values from -6 to 6
- lengths: int32 [16], P('dp'), may hold values from 192 to 1536, as said below
- cotangent: bfloat16 [16, 1536, 768], P('dp'), may hold values from -6 to 6
- norm1_gain: float32 [768], replicated, may hold values from 0.1 to 1.9
- norm1_bias: float32 [768], replicated, may hold values from -3 to 3
- query_weight: bfloat16 [768, 768], P(None, 'tensor'), may hold values from -0.21875 to 0.21875
- query_bias: float32 [768], P('tensor'), may hold values from -3 to 3
- key_weight: bfloat16 [768, 768], P(None, 'tensor'), may hold values from -0.21875 to 0.21875
- value_weight: bfloat16 [768, 768], P(None, 'tensor'), may hold values from -0.21875 to 0.21875
- value_bias: float32 [768], P('tensor'), may hold values from -3 to 3
- output_weight: bfloat16 [768, 768], P('tensor'), may hold values from -0.875 to 0.875
- output_bias: float32 [768], replicated, may hold values from -3 to 3
- norm2_gain: float32 [768], replicated, may hold values from 0.1 to 1.9
- norm2_bias: float32 [768], replicated, may hold values from -3 to 3
- hidden_weight: bfloat16 [768, 3072], P(None, 'tensor'), may hold values from -0.21875 to 0.21875
- hidden_bias: float32 [3072], P('tensor'), may hold values from -3 to 3
- proj_weight: bfloat16 [3072, 768], P('tensor'), may hold values from -0.15625 to 0.15625
- proj_bias: float32 [768], replicated, may hold values from -3 to 3
Outputs:
- block_out: bfloat16 [16, 1536, 768], P('dp')
- input_grad: bfloat16 [16, 1536, 768], P('dp')
- grad_norm1_gain: float32 [768], replicated
- grad_norm1_bias: float32 [768], replicated
- grad_query_weight: float32 [768, 768], P(None, 'tensor')
- grad_query_bias: float32 [768], P('tensor')
- grad_key_weight: float32 [768, 768], P(None, 'tensor')
- grad_value_weight: float32 [768, 768], P(None, 'tensor')
- grad_value_bias: float32 [768], P('tensor')
- grad_output_weight: float32 [768, 768], P('tensor')
- grad_output_bias: float32 [768], replicated
- grad_norm2_gain: float32 [768], replicated
- grad_norm2_bias: float32 [768], replicated
- grad_hidden_weight: float32 [768, 3072], P(None, 'tensor')
- grad_hidden_bias: float32 [3072], P('tensor')
- grad_proj_weight: float32 [3072, 768], P('tensor')
- grad_proj_bias: float32 [768], replicated
Inputs may be any that keep to these rules, and one draw needn't show every extreme that they name: `lengths`: valid frames of each clip; positions at or beyond it are padding that no key attention reads and that carry no loss; some clip has exactly 1536.
All inputs are finite; a program needn't handle non-finite values.
Results may differ from a plain program's by a relative error of at most 0.013.
The roundings to bfloat16 on the way count: a program that leaves them out, or rounds other values in their place, can miss the bound.
Values sent between devices are 32-bit elements; how exact they have to be, the bound alone decides.
A program may use at most 192 MiB of HBM per device.

v0:
```python
import math

import jax
import jax.numpy as jnp
from jax import lax
from jax.sharding import PartitionSpec as P

HD = 64


eps = 1e-05
score_scale = 0.125
masked_value = -1e30


def contract(form, left, right):
    return jnp.einsum(form, left, right, preferred_element_type=jnp.float32)


def mat_dot(left, right):
    return jnp.dot(left, right, preferred_element_type=jnp.float32)


def layer_norm(values_in, norm_gain, norm_shift):
    center = values_in - jnp.mean(values_in, axis=-1, keepdims=True)
    inverse = lax.rsqrt(jnp.mean(center * center, axis=-1, keepdims=True) + eps)
    unit_rows = center * inverse
    return (unit_rows * norm_gain + norm_shift, unit_rows, inverse)


def norm_back(grad_rows, unit_rows, inverse, norm_gain):
    scaled = grad_rows * norm_gain
    return inverse * (
        scaled
        - jnp.mean(scaled, axis=-1, keepdims=True)
        - unit_rows * jnp.mean(scaled * unit_rows, axis=-1, keepdims=True)
    )


def gelu_parts(before):
    normal_cdf = 0.5 * (1.0 + jax.scipy.special.erf(before * (1.0 / math.sqrt(2.0))))
    return (
        before * normal_cdf,
        normal_cdf + before * jnp.exp(-0.5 * before * before) * (1.0 / math.sqrt(2.0 * math.pi)),
    )


def attend_forward(queries, keys_in, values_in, clip_length):
    total_rows, head_count, head_size = queries.shape
    block_rows = min(512, total_rows)
    live_keys = jnp.arange(total_rows) < clip_length

    def per_block(query_block):
        scores = contract("qhd,khd->hqk", query_block, keys_in)
        scores = jnp.where(live_keys[None, None, :], scores, masked_value)
        maxima = jnp.max(scores, axis=-1, keepdims=True)
        exponent = jnp.exp(scores - maxima)
        totals = jnp.sum(exponent, axis=-1, keepdims=True)
        weights = (exponent / totals).astype(jnp.bfloat16)
        mixture = contract("hqk,khd->qhd", weights, values_in).astype(jnp.bfloat16)
        return (mixture, (maxima + jnp.log(totals))[..., 0])

    mixture, log_sums = lax.map(
        per_block, queries.reshape(total_rows // block_rows, block_rows, head_count, head_size)
    )
    return (mixture.reshape(total_rows, head_count, head_size), log_sums)


def attend_backward(queries, keys_in, values_in, attended, grad_attended, log_sums, clip_length):
    total_rows, head_count, head_size = queries.shape
    block_rows = min(512, total_rows)
    blocks = total_rows // block_rows
    live_keys = jnp.arange(total_rows) < clip_length
    deltas = jnp.sum(grad_attended.astype(jnp.float32) * attended.astype(jnp.float32), axis=-1)

    def per_block(carry, inputs):
        query_block, grad_block, delta_block, log_block = inputs
        scores = contract("qhd,khd->hqk", query_block, keys_in)
        scores = jnp.where(live_keys[None, None, :], scores, masked_value)
        probs = jnp.exp(scores - log_block[..., None])
        grad_probs = contract("qhd,khd->hqk", grad_block, values_in)
        grad_scores = (probs * (grad_probs - jnp.transpose(delta_block)[..., None])).astype(
            jnp.bfloat16
        )
        grad_query = contract("hqk,khd->qhd", grad_scores, keys_in) * score_scale
        grad_keys = carry[0] + contract("hqk,qhd->khd", grad_scores, query_block)
        grad_values = carry[1] + contract("hqk,qhd->khd", probs.astype(jnp.bfloat16), grad_block)
        return ((grad_keys, grad_values), grad_query)

    start = jnp.zeros((total_rows, head_count, head_size), jnp.float32)
    (grad_keys, grad_values), grad_query = lax.scan(
        per_block,
        (start, start),
        (
            queries.reshape(blocks, block_rows, head_count, head_size),
            grad_attended.reshape(blocks, block_rows, head_count, head_size),
            deltas.reshape(blocks, block_rows, head_count),
            log_sums,
        ),
    )
    return (grad_query.reshape(total_rows, head_count, head_size), grad_keys, grad_values)


def on_device(
    frames,
    lengths,
    cotangent,
    norm1_gain,
    norm1_bias,
    query_weight,
    query_bias,
    key_weight,
    value_weight,
    value_bias,
    output_weight,
    output_bias,
    norm2_gain,
    norm2_bias,
    hidden_weight,
    hidden_bias,
    proj_weight,
    proj_bias,
):
    clip_length = lengths[0]
    total_rows = frames.shape[1]
    head_count = query_weight.shape[1] // HD
    head_shape = (total_rows, head_count, HD)
    inputs_f = frames[0].astype(jnp.float32)
    normed_one, unit_one, inverse_one = layer_norm(inputs_f, norm1_gain, norm1_bias)
    first_in = normed_one.astype(jnp.bfloat16)
    queries = ((mat_dot(first_in, query_weight) + query_bias) * score_scale).astype(jnp.bfloat16)
    keys_in = mat_dot(first_in, key_weight).astype(jnp.bfloat16)
    values_in = (mat_dot(first_in, value_weight) + value_bias).astype(jnp.bfloat16)
    attended, log_sums = attend_forward(
        queries.reshape(head_shape),
        keys_in.reshape(head_shape),
        values_in.reshape(head_shape),
        clip_length,
    )
    attended_flat = attended.reshape(total_rows, head_count * HD)
    attn_total = lax.psum(mat_dot(attended_flat, output_weight), "tensor")
    resid = inputs_f + attn_total + output_bias
    normed_two, unit_two, inverse_two = layer_norm(resid, norm2_gain, norm2_bias)
    second_in = normed_two.astype(jnp.bfloat16)
    before = mat_dot(second_in, hidden_weight) + hidden_bias
    active_f, slope = gelu_parts(before)
    active = active_f.astype(jnp.bfloat16)
    mlp_total = lax.psum(mat_dot(active, proj_weight), "tensor")
    block_out = (resid + mlp_total + proj_bias).astype(jnp.bfloat16)
    live_rows = (jnp.arange(total_rows) < clip_length)[:, None]
    grad_raw = cotangent[0]
    grad_clip = jnp.where(live_rows, grad_raw, jnp.zeros_like(grad_raw))
    grad_f = grad_clip.astype(jnp.float32)
    g_proj_b = jnp.sum(grad_f, axis=0)
    g_proj_w = mat_dot(active.T, grad_clip)
    grad_pre = mat_dot(grad_clip, proj_weight.T) * slope
    g_hidden_b = jnp.sum(grad_pre, axis=0)
    grad_pre_b = grad_pre.astype(jnp.bfloat16)
    g_hidden_w = mat_dot(second_in.T, grad_pre_b)
    grad_two = lax.psum(mat_dot(grad_pre_b, hidden_weight.T), "tensor")
    g_norm2_gain = jnp.sum(grad_two * unit_two, axis=0)
    g_norm2_bias = jnp.sum(grad_two, axis=0)
    grad_resid = grad_f + norm_back(grad_two, unit_two, inverse_two, norm2_gain)
    g_output_b = jnp.sum(grad_resid, axis=0)
    grad_resid_b = grad_resid.astype(jnp.bfloat16)
    g_output_w = mat_dot(attended_flat.T, grad_resid_b)
    grad_attended = mat_dot(grad_resid_b, output_weight.T).astype(jnp.bfloat16)
    grad_query, grad_key, grad_value = attend_backward(
        queries.reshape(head_shape),
        keys_in.reshape(head_shape),
        values_in.reshape(head_shape),
        attended,
        grad_attended.reshape(head_shape),
        log_sums,
        clip_length,
    )
    grad_query = grad_query.reshape(total_rows, head_count * HD)
    grad_key = grad_key.reshape(total_rows, head_count * HD)
    grad_value = grad_value.reshape(total_rows, head_count * HD)
    g_query_b = jnp.sum(grad_query, axis=0)
    g_value_b = jnp.sum(grad_value, axis=0)
    query_g_b = grad_query.astype(jnp.bfloat16)
    key_g_b = grad_key.astype(jnp.bfloat16)
    value_g_b = grad_value.astype(jnp.bfloat16)
    g_query_w = mat_dot(first_in.T, query_g_b)
    g_key_w = mat_dot(first_in.T, key_g_b)
    g_value_w = mat_dot(first_in.T, value_g_b)
    partial_one = (
        mat_dot(query_g_b, query_weight.T)
        + mat_dot(key_g_b, key_weight.T)
        + mat_dot(value_g_b, value_weight.T)
    )
    grad_one = lax.psum(partial_one, "tensor")
    g_norm1_gain = jnp.sum(grad_one * unit_one, axis=0)
    g_norm1_bias = jnp.sum(grad_one, axis=0)
    input_grad = (grad_resid + norm_back(grad_one, unit_one, inverse_one, norm1_gain)).astype(
        jnp.bfloat16
    )
    summed = lax.psum(
        (
            g_norm1_gain,
            g_norm1_bias,
            g_query_w,
            g_query_b,
            g_key_w,
            g_value_w,
            g_value_b,
            g_output_w,
            g_output_b,
            g_norm2_gain,
            g_norm2_bias,
            g_hidden_w,
            g_hidden_b,
            g_proj_w,
            g_proj_b,
        ),
        "dp",
    )
    (
        s_norm1_gain,
        s_norm1_bias,
        s_query_w,
        s_query_b,
        s_key_w,
        s_value_w,
        s_value_b,
        s_output_w,
        s_output_b,
        s_norm2_gain,
        s_norm2_bias,
        s_hidden_w,
        s_hidden_b,
        s_proj_w,
        s_proj_b,
    ) = summed
    return (
        block_out[None],
        input_grad[None],
        s_norm1_gain,
        s_norm1_bias,
        s_query_w,
        s_query_b,
        s_key_w,
        s_value_w,
        s_value_b,
        s_output_w,
        s_output_b,
        s_norm2_gain,
        s_norm2_bias,
        s_hidden_w,
        s_hidden_b,
        s_proj_w,
        s_proj_b,
    )


def solution(mesh):
    placed = (
        P("dp", None, None),
        P("dp"),
        P("dp", None, None),
        P(),
        P(),
        P(None, "tensor"),
        P("tensor"),
        P(None, "tensor"),
        P(None, "tensor"),
        P("tensor"),
        P("tensor", None),
        P(),
        P(),
        P(),
        P(None, "tensor"),
        P("tensor"),
        P("tensor", None),
        P(),
    )
    return jax.shard_map(
        on_device,
        mesh=mesh,
        in_specs=placed,
        out_specs=(
            P("dp", None, None),
            P("dp", None, None),
            P(),
            P(),
            P(None, "tensor"),
            P("tensor"),
            P(None, "tensor"),
            P(None, "tensor"),
            P("tensor"),
            P("tensor", None),
            P(),
            P(),
            P(),
            P(None, "tensor"),
            P("tensor"),
            P("tensor", None),
            P(),
        ),
        check_vma=False,
    )
```

profile of v0, /device:TPU:0, one launch (start us, length us, event | category | flops | bytes accessed | tf_op | source)
XLA Modules:
  0.0 867.2 jit_solution(5801638124540104245)
XLA Ops:
  9.5 2.5 fusion.63
  16.2 3.1 reshape.223
  19.3 4.4 copy.39
  23.7 2.9 convolution_convert_fusion.1
  26.6 3.9 fusion.71
  30.5 92.7 %while.28 = (s32[]{:T(128)}, bf16[3,512,6,64]{1,3,2,0:T(8,128)(2,1)}, f32[3,6,512]{2,1,0:T(8,128)}, bf16[3,512,6,64]{1,3,2,0:T(8,128)(2,1)}, bf16[1536,6,64]{0,2...) while((s32[]{:T(128)}, bf16[3,512,6,64]{1,3,2,0:T(8,128)(2,1)}, ...), condition=%wide.region_5.6_spmd.clone, body=%wide.region_2.5_spmd.clone.sunk | while | flops 1250621952 | bytes 59893876 | solution.py:63
  31.2 9.1 %select_reduce_fusion.2 = (f32[6,512]{1,0:T(8,128)S(1)}, f32[6,512,1536]{2,1,0:T(8,128)}) fusion(pred[1536]{0:T(1024)(128)(4,1)S(1)} %iota_compare_fusion.5, bf16[1536,6,64]{0,2,1:T(8,128)(2,1)S(1)} %get-tuple-element.425, bf16[3,512,6,64]{1,3,2,0:T(8,128)(2,1)} %get-tuple-element.424, s32[]{:T(128)} %get-tuple-element.413), kind=kOutput, calls=%fused_computation.4.clone.1 | convolution fusion | flops 613413888 | bytes 20461568 | tf_op jit(solution)/shard_map/while/body/eval_jaxpr/qhd,khd->hqk/dot_general | solution.py:17
  40.3 10.2 %fusion.154 = f32[6,512]{1,0:T(8,128)} fusion(f32[6,512,1536]{2,1,0:T(8,128)} %get-tuple-element.392, f32[6,512]{1,0:T(8,128)S(1)} %get-tuple-element.393, pred[1536]{0:T(1024)(128)(4,1)} %copy-done.23), kind=kLoop, calls=%fused_computation.5.clone.1 | loop fusion | flops 14152704 | bytes 18900480 | tf_op jit(solution)/shard_map/while/body/eval_jaxpr/reduce_sum | solution.py:58
  51.8 9.5 %fusion.155 = bf16[3,512,6,64]{1,3,2,0:T(8,128)(2,1)} fusion(bf16[3,512,6,64]{1,3,2,0:T(8,128)(2,1)} %get-tuple-element.414, s32[]{:T(128)} %get-tuple-element.413, bf16[1536,6,64]{0,2,1:T(8,128)(2,1)} %get-tuple-element.426, f32[6,512,1536]{2,1,0:T(8,128)} %get-tuple-element.392, f32[6,512]{1,0:T(8,128)} %fusion.154, ...), kind=kOutput, calls=%fused_computation.9.clone.1 | convolution fusion | flops 623050752 | bytes 20478464 | tf_op jit(solution)/shard_map/while/body/eval_jaxpr/hqk,khd->qhd/dot_general | solution.py:17
  62.0 9.2 %select_reduce_fusion.2 = (f32[6,512]{1,0:T(8,128)S(1)}, f32[6,512,1536]{2,1,0:T(8,128)}) fusion(pred[1536]{0:T(1024)(128)(4,1)S(1)} %iota_compare_fusion.5, bf16[1536,6,64]{0,2,1:T(8,128)(2,1)S(1)} %get-tuple-element.425, bf16[3,512,6,64]{1,3,2,0:T(8,128)(2,1)} %get-tuple-element.424, s32[]{:T(128)} %get-tuple-element.413), kind=kOutput, calls=%fused_computation.4.clone.1 | convolution fusion | flops 613413888 | bytes 20461568 | tf_op jit(solution)/shard_map/while/body/eval_jaxpr/qhd,khd->hqk/dot_general | solution.py:17
  71.1 10.2 %fusion.154 = f32[6,512]{1,0:T(8,128)} fusion(f32[6,512,1536]{2,1,0:T(8,128)} %get-tuple-element.392, f32[6,512]{1,0:T(8,128)S(1)} %get-tuple-element.393, pred[1536]{0:T(1024)(128)(4,1)} %copy-done.23), kind=kLoop, calls=%fused_computation.5.clone.1 | loop fusion | flops 14152704 | bytes 18900480 | tf_op jit(solution)/shard_map/while/body/eval_jaxpr/reduce_sum | solution.py:58
  82.7 9.5 %fusion.155 = bf16[3,512,6,64]{1,3,2,0:T(8,128)(2,1)} fusion(bf16[3,512,6,64]{1,3,2,0:T(8,128)(2,1)} %get-tuple-element.414, s32[]{:T(128)} %get-tuple-element.413, bf16[1536,6,64]{0,2,1:T(8,128)(2,1)} %get-tuple-element.426, f32[6,512,1536]{2,1,0:T(8,128)} %get-tuple-element.392, f32[6,512]{1,0:T(8,128)} %fusion.154, ...), kind=kOutput, calls=%fused_computation.9.clone.1 | convolution fusion | flops 623050752 | bytes 20478464 | tf_op jit(solution)/shard_map/while/body/eval_jaxpr/hqk,khd->qhd/dot_general | solution.py:17
  92.8 9.2 %select_reduce_fusion.2 = (f32[6,512]{1,0:T(8,128)S(1)}, f32[6,512,1536]{2,1,0:T(8,128)}) fusion(pred[1536]{0:T(1024)(128)(4,1)S(1)} %iota_compare_fusion.5, bf16[1536,6,64]{0,2,1:T(8,128)(2,1)S(1)} %get-tuple-element.425, bf16[3,512,6,64]{1,3,2,0:T(8,128)(2,1)} %get-tuple-element.424, s32[]{:T(128)} %get-tuple-element.413), kind=kOutput, calls=%fused_computation.4.clone.1 | convolution fusion | flops 613413888 | bytes 20461568 | tf_op jit(solution)/shard_map/while/body/eval_jaxpr/qhd,khd->hqk/dot_general | solution.py:17
  101.9 10.2 %fusion.154 = f32[6,512]{1,0:T(8,128)} fusion(f32[6,512,1536]{2,1,0:T(8,128)} %get-tuple-element.392, f32[6,512]{1,0:T(8,128)S(1)} %get-tuple-element.393, pred[1536]{0:T(1024)(128)(4,1)} %copy-done.23), kind=kLoop, calls=%fused_computation.5.clone.1 | loop fusion | flops 14152704 | bytes 18900480 | tf_op jit(solution)/shard_map/while/body/eval_jaxpr/reduce_sum | solution.py:58
  113.5 9.5 %fusion.155 = bf16[3,512,6,64]{1,3,2,0:T(8,128)(2,1)} fusion(bf16[3,512,6,64]{1,3,2,0:T(8,128)(2,1)} %get-tuple-element.414, s32[]{:T(128)} %get-tuple-element.413, bf16[1536,6,64]{0,2,1:T(8,128)(2,1)} %get-tuple-element.426, f32[6,512,1536]{2,1,0:T(8,128)} %get-tuple-element.392, f32[6,512]{1,0:T(8,128)} %fusion.154, ...), kind=kOutput, calls=%fused_computation.9.clone.1 | convolution fusion | flops 623050752 | bytes 20478464 | tf_op jit(solution)/shard_map/while/body/eval_jaxpr/hqk,khd->qhd/dot_general | solution.py:17
  123.3 2.3 copy.40
  127.1 3.6 fusion.90
  132.0 30.7 %all-reduce.8.cloned.1.call-done = f32[1536,768]{1,0:T(8,128)} async-done(((f32[1536,768]{1,0:T(8,128)}), f32[1536,768]{1,0:T(8,128)}) %all-reduce.8.cloned.1.call-update) | async-done | bytes 4718608 | tf_op jit(solution)/shard_map/psum | solution.py:141
  162.7 3.8 fusion.85
  167.4 6.4 multiply_convert_fusion.1
  173.8 7.4 fusion.89
  183.3 5.5 fusion.78
  192.4 8.7 fusion.91
  201.0 18.3 %all-reduce.10.cloned.1.call-done = f32[1536,768]{1,0:T(8,128)} async-done(((f32[1536,768]{1,0:T(8,128)}), f32[1536,768]{1,0:T(8,128)}) %all-reduce.10.cloned.1.call-update) | async-done | bytes 4718608 | tf_op jit(solution)/shard_map/psum | solution.py:160
  219.3 5.8 multiply_reduce_fusion
  225.2 5.1 fusion.84
  230.4 2.2 copy-done.6
  234.7 3.8 reshape_reshape.13
  238.5 2.7 copy.43
  241.2 3.0 fusion.75
  244.2 136.3 %while.29 = (s32[]{:T(128)}, f32[1536,6,64]{0,2,1:T(8,128)S(1)}, f32[1536,6,64]{0,2,1:T(8,128)}, f32[3,512,6,64]{1,3,2,0:T(8,128)}, bf16[3,512,6,64]{1,3,2,0:T(8...) while((s32[]{:T(128)}, f32[1536,6,64]{0,2,1:T(8,128)S(1)}, ...), condition=%wide.region_15.16_spmd.clone, body=%wide.region_14.15_spmd.clone.sunk | while | flops 3060205056 | bytes 142843152 | solution.py:91
  244.2 9.2 %fusion.166 = f32[6,512,1536]{2,1,0:T(8,128)} fusion(bf16[1536,6,64]{0,2,1:T(8,128)(2,1)S(1)} %get-tuple-element.460, bf16[3,512,6,64]{1,3,2,0:T(8,128)(2,1)} %get-tuple-element.459, s32[]{:T(128)} %get-tuple-element.442), kind=kOutput, calls=%fused_computation.34.clone.1 | convolution fusion | flops 603979776 | bytes 20447744 | tf_op jit(solution)/shard_map/while/body/eval_jaxpr/qhd,khd->hqk/dot_general | solution.py:17
  256.1 11.2 %multiply_convert_fusion.3 = bf16[6,512,1536]{2,1,0:T(8,128)(2,1)} fusion(f32[6,512,1536]{2,1,0:T(8,128)} %fusion.166, f32[6,512]{1,0:T(8,128)S(1)} %dynamic-slice_bitcast_fusion.4, f32[6,512]{1,0:T(8,128)S(1)} %dynamic-slice_bitcast_fusion.5, pred[1536]{0:T(1024)(128)(4,1)S(1)} %iota_compare_fusion.6, bf16[1536,6,64]{0,2,1:T(8,128)(2,1)S(1)} %copy-done.63, ...), kind=kOutput, calls=%fused_computation.17.clone.1 | convolution fusion | flops 627572736 | bytes 29911040 | tf_op jit(solution)/shard_map/while/body/eval_jaxpr/qhd,khd->hqk/dot_general | solution.py:17
  267.3 5.8 fusion.167
  273.8 3.9 fusion.169
  277.7 11.4 %fusion.168 = f32[1536,6,64]{0,2,1:T(8,128)} fusion(f32[6,512,1536]{2,1,0:T(8,128)} %fusion.166, f32[6,512]{1,0:T(8,128)S(1)} %dynamic-slice_bitcast_fusion.5, pred[1536]{0:T(1024)(128)(4,1)S(1)} %copy-done.31, f32[1536,6,64]{0,2,1:T(8,128)} %get-tuple-element.444, pred[]{:T(512)S(6)} %compare.3, bf16[3,512,6,64]{1,3,2,0:T(8,128)(2,1)} %get-tuple-element.462, ...), kind=kOutput, calls=%fused_computation.25.clone.1 | convolution fusion | flops 619315200 | bytes 24000512 | tf_op jit(solution)/shard_map/while/body/eval_jaxpr/hqk,qhd->khd/dot_general | solution.py:17
  289.1 9.2 %fusion.166 = f32[6,512,1536]{2,1,0:T(8,128)} fusion(bf16[1536,6,64]{0,2,1:T(8,128)(2,1)S(1)} %get-tuple-element.460, bf16[3,512,6,64]{1,3,2,0:T(8,128)(2,1)} %get-tuple-element.459, s32[]{:T(128)} %get-tuple-element.442), kind=kOutput, calls=%fused_computation.34.clone.1 | convolution fusion | flops 603979776 | bytes 20447744 | tf_op jit(solution)/shard_map/while/body/eval_jaxpr/qhd,khd->hqk/dot_general | solution.py:17
  301.0 11.2 %multiply_convert_fusion.3 = bf16[6,512,1536]{2,1,0:T(8,128)(2,1)} fusion(f32[6,512,1536]{2,1,0:T(8,128)} %fusion.166, f32[6,512]{1,0:T(8,128)S(1)} %dynamic-slice_bitcast_fusion.4, f32[6,512]{1,0:T(8,128)S(1)} %dynamic-slice_bitcast_fusion.5, pred[1536]{0:T(1024)(128)(4,1)S(1)} %iota_compare_fusion.6, bf16[1536,6,64]{0,2,1:T(8,128)(2,1)S(1)} %copy-done.63, ...), kind=kOutput, calls=%fused_computation.17.clone.1 | convolution fusion | flops 627572736 | bytes 29911040 | tf_op jit(solution)/shard_map/while/body/eval_jaxpr/qhd,khd->hqk/dot_general | solution.py:17
  312.2 5.8 fusion.167
  318.7 3.9 fusion.169
  322.6 12.1 %fusion.168 = f32[1536,6,64]{0,2,1:T(8,128)} fusion(f32[6,512,1536]{2,1,0:T(8,128)} %fusion.166, f32[6,512]{1,0:T(8,128)S(1)} %dynamic-slice_bitcast_fusion.5, pred[1536]{0:T(1024)(128)(4,1)S(1)} %copy-done.31, f32[1536,6,64]{0,2,1:T(8,128)} %get-tuple-element.444, pred[]{:T(512)S(6)} %compare.3, bf16[3,512,6,64]{1,3,2,0:T(8,128)(2,1)} %get-tuple-element.462, ...), kind=kOutput, calls=%fused_computation.25.clone.1 | convolution fusion | flops 619315200 | bytes 24000512 | tf_op jit(solution)/shard_map/while/body/eval_jaxpr/hqk,qhd->khd/dot_general | solution.py:17
  334.7 9.2 %fusion.166 = f32[6,512,1536]{2,1,0:T(8,128)} fusion(bf16[1536,6,64]{0,2,1:T(8,128)(2,1)S(1)} %get-tuple-element.460, bf16[3,512,6,64]{1,3,2,0:T(8,128)(2,1)} %get-tuple-element.459, s32[]{:T(128)} %get-tuple-element.442), kind=kOutput, calls=%fused_computation.34.clone.1 | convolution fusion | flops 603979776 | bytes 20447744 | tf_op jit(solution)/shard_map/while/body/eval_jaxpr/qhd,khd->hqk/dot_general | solution.py:17
  346.6 11.2 %multiply_convert_fusion.3 = bf16[6,512,1536]{2,1,0:T(8,128)(2,1)} fusion(f32[6,512,1536]{2,1,0:T(8,128)} %fusion.166, f32[6,512]{1,0:T(8,128)S(1)} %dynamic-slice_bitcast_fusion.4, f32[6,512]{1,0:T(8,128)S(1)} %dynamic-slice_bitcast_fusion.5, pred[1536]{0:T(1024)(128)(4,1)S(1)} %iota_compare_fusion.6, bf16[1536,6,64]{0,2,1:T(8,128)(2,1)S(1)} %copy-done.63, ...), kind=kOutput, calls=%fused_computation.17.clone.1 | convolution fusion | flops 627572736 | bytes 29911040 | tf_op jit(solution)/shard_map/while/body/eval_jaxpr/qhd,khd->hqk/dot_general | solution.py:17
  357.8 5.8 fusion.167
  364.3 3.8 fusion.169
  368.2 12.1 %fusion.168 = f32[1536,6,64]{0,2,1:T(8,128)} fusion(f32[6,512,1536]{2,1,0:T(8,128)} %fusion.166, f32[6,512]{1,0:T(8,128)S(1)} %dynamic-slice_bitcast_fusion.5, pred[1536]{0:T(1024)(128)(4,1)S(1)} %copy-done.31, f32[1536,6,64]{0,2,1:T(8,128)} %get-tuple-element.444, pred[]{:T(512)S(6)} %compare.3, bf16[3,512,6,64]{1,3,2,0:T(8,128)(2,1)} %get-tuple-element.462, ...), kind=kOutput, calls=%fused_computation.25.clone.1 | convolution fusion | flops 619315200 | bytes 24000512 | tf_op jit(solution)/shard_map/while/body/eval_jaxpr/hqk,qhd->khd/dot_general | solution.py:17
  380.5 3.3 fusion.88
  385.2 3.6 fusion.87
  391.9 3.7 add_add_fusion
  397.2 2.3 fusion.73
  399.6 10.3 %fusion.83 = f32[1536,768]{1,0:T(8,128)} fusion(bf16[1536,1536]{1,0:T(8,128)(2,1)} %get-tuple-element.283, bf16[1,1536,768]{2,1,0:T(8,128)(2,1)} %param.24, pred[1536]{0:T(1024)(128)(4,1)S(1)} %copy-done.52), kind=kOutput, calls=%fused_computation.123 | convolution fusion | flops 3625058304 | bytes 11798016 | tf_op jit(solution)/shard_map/dot_general | solution.py:21
  410.0 6.0 fusion.76
  416.0 2.4 fusion.94
  418.4 2.4 fusion.96
  420.9 2.4 fusion.95
  426.3 11.4 %all-reduce.14.cloned.1.call-done = (f32[1536,768]{1,0:T(8,128)}, f32[1536,768]{1,0:T(8,128)}) async-done(((f32[1536,768]{1,0:T(8,128)}, f32[1536,768]{1,0:T(8,128)}), (f32[1536,768]{1,0:T(8,128)}, f32[1536,768]{1,0:T(8,128)})) %all-reduce.14.cloned.1.call-update) | async-done | bytes 9437200 | tf_op jit(solution)/shard_map/psum | solution.py:148
  437.7 4.0 fusion.62
  441.7 82.2 %all-reduce = (f32[768]{0:T(1024)}, f32[768]{0:T(1024)}, f32[384]{0:T(512)}, f32[384]{0:T(512)}, f32[768]{0:T(1024)}, /*index=5*/f32[768]{0:T(1024)}, f32[768]{0:T(1024)}, f32[1536]{0:T(1024)}, f32[768]{0:T(1024)}) all-reduce(f32[768]{0:T(1024)S(1)} %get-tuple-element.213, ...), channel_id=1, replica_groups=mesh['dp'=16,'tensor'=2] {'dp'}, use_global_device_ids=true, to_apply=%region_20.21 | all-reduce | flops 6912 | bytes 55296 | tf_op jit(solution)/shard_map/psum | solution.py:199
  524.0 6.4 fusion.72
  531.9 2.8 fusion.74
  534.7 312.4 %all-reduce.12.cloned.1.call-done = (f32[768,384]{1,0:T(8,128)}, f32[768,384]{1,0:T(8,128)}, f32[768,384]{1,0:T(8,128)}, f32[384,768]{1,0:T(8,128)}, f32[768,1536]{1,0:T(8,128)}, /*index=5*/f32[1536,768]{1,0:T(8,128)}) async-done(((f32[768,384]{1,0:T(8,128)}, f32[768,384]{1,0:T(8,128)}, f32[768,384]{1,0:T(8,128)}, f32[384,768]{1,0:T(8,128)}, f32[768,1536]{1,0:T(8,128)}, /*index=5*/f32[1536,768]{1,0:T(8,128)}), ...) | async-done | bytes 14155792 | tf_op jit(solution)/shard_map/psum | solution.py:199
  847.2 2.5 copy.85
  849.7 2.7 copy.86
  854.4 2.4 copy.89
  (229 shorter events, 49.0 us)
Async XLA Ops:
  7.2 160.1 %copy-start = (bf16[768,1536]{1,0:T(8,128)(2,1)S(1)}, bf16[768,1536]{1,0:T(8,128)(2,1)}, u32[]{:S(2)}) copy-start(bf16[768,1536]{1,0:T(8,128)(2,1)} %param.36) | copy-start | bytes 7077892
  7.2 4.9 copy-start.38
  7.2 4.9 copy-start.45
  7.2 155.5 %all-reduce.8.cloned.1.call-start = ((), (), s32[]{:S(2)}) async-start(), calls=%async_computation | async-start | bytes 9437184 | tf_op jit(solution)/shard_map/psum | solution.py:141
  7.3 4.8 copy-start.4
  7.3 7.5 copy-start.24
  7.3 7.4 copy-start.61
  19.3 7.3 copy-start.62
  31.2 9.2 %copy-start.23 = (pred[1536]{0:T(1024)(128)(4,1)}, pred[1536]{0:T(1024)(128)(4,1)S(1)}, u32[]{:S(2)}) copy-start(pred[1536]{0:T(1024)(128)(4,1)S(1)} %iota_compare_fusion.5) | copy-start | bytes 4612 | tf_op jit(solution)/shard_map/while
  62.0 9.2 %copy-start.23 = (pred[1536]{0:T(1024)(128)(4,1)}, pred[1536]{0:T(1024)(128)(4,1)S(1)}, u32[]{:S(2)}) copy-start(pred[1536]{0:T(1024)(128)(4,1)S(1)} %iota_compare_fusion.5) | copy-start | bytes 4612 | tf_op jit(solution)/shard_map/while
  92.8 9.2 %copy-start.23 = (pred[1536]{0:T(1024)(128)(4,1)}, pred[1536]{0:T(1024)(128)(4,1)S(1)}, u32[]{:S(2)}) copy-start(pred[1536]{0:T(1024)(128)(4,1)S(1)} %iota_compare_fusion.5) | copy-start | bytes 4612 | tf_op jit(solution)/shard_map/while
  130.7 32.0 %copy-start.54 = (f32[768]{0:T(1024)S(1)}, f32[768]{0:T(1024)}, u32[]{:S(2)}) copy-start(f32[768]{0:T(1024)} %param.33) | copy-start | bytes 9220
  130.7 88.6 %all-reduce.10.cloned.1.call-start = ((), (), s32[]{:S(2)}) async-start(), calls=%async_computation.1 | async-start | bytes 9437184 | tf_op jit(solution)/shard_map/psum | solution.py:160
  166.5 7.3 copy-start.3
  166.6 58.6 %copy-start.34 = (f32[1536]{0:T(1024)}, f32[1536]{0:T(1024)S(1)}, u32[]{:S(2)}) copy-start(f32[1536]{0:T(1024)S(1)} %broadcast_multiply_fusion.4) | copy-start | bytes 18436
  167.3 57.8 %copy-start.36 = (f32[1536]{0:T(1024)}, f32[1536]{0:T(1024)S(1)}, u32[]{:S(2)}) copy-start(f32[1536]{0:T(1024)S(1)} %add_rsqrt_fusion) | copy-start | bytes 18436
  167.3 6.4 copy-start.16
  167.3 6.4 copy-start.50
  167.3 6.4 copy-start.56
  188.8 248.8 %all-reduce.14.cloned.1.call-start = ((), (), s32[]{:S(2)}) async-start(), calls=%async_computation.3 | async-start | bytes 18874368 | tf_op jit(solution)/shard_map/psum | solution.py:148
  219.3 5.8 copy-start.7
  219.3 5.9 copy-start.17
  219.3 5.9 copy-start.41
  219.3 5.9 copy-start.51
  225.2 7.3 copy-start.19
  244.2 11.9 %copy-start.63 = (bf16[1536,6,64]{0,2,1:T(8,128)(2,1)S(1)}, bf16[1536,6,64]{0,2,1:T(8,128)(2,1)}, u32[]{:S(2)}) copy-start(bf16[1536,6,64]{0,2,1:T(8,128)(2,1)} %get-tuple-element.463) | copy-start | bytes 3538948 | tf_op jit(solution)/shard_map/while
  267.3 6.5 copy-start.2
  273.8 3.9 copy-start.31
  289.1 11.9 %copy-start.63 = (bf16[1536,6,64]{0,2,1:T(8,128)(2,1)S(1)}, bf16[1536,6,64]{0,2,1:T(8,128)(2,1)}, u32[]{:S(2)}) copy-start(bf16[1536,6,64]{0,2,1:T(8,128)(2,1)} %get-tuple-element.463) | copy-start | bytes 3538948 | tf_op jit(solution)/shard_map/while
  312.2 6.5 copy-start.2
  318.7 3.9 copy-start.31
  334.7 11.9 %copy-start.63 = (bf16[1536,6,64]{0,2,1:T(8,128)(2,1)S(1)}, bf16[1536,6,64]{0,2,1:T(8,128)(2,1)}, u32[]{:S(2)}) copy-start(bf16[1536,6,64]{0,2,1:T(8,128)(2,1)} %get-tuple-element.463) | copy-start | bytes 3538948 | tf_op jit(solution)/shard_map/while
  357.8 6.5 copy-start.2
  364.3 3.9 copy-start.31
  384.8 4.2 copy-start.25
  385.2 5.2 copy-start.9
  395.6 451.6 %all-reduce.12.cloned.1.call-start = ((), (), s32[]{:S(2)}) async-start(), calls=%async_computation.2 | async-start | bytes 28311552 | tf_op jit(solution)/shard_map/psum | solution.py:199
  397.2 12.7 %slice-start = ((s8[4718592]{0:T(1024)(128)(4,1)}), s8[4194304]{0:T(1024)(128)(4,1)S(1)}, s32[]{:S(2)}) async-start(s8[4718592]{0:T(1024)(128)(4,1)} %bitcast.201), calls=%async_computation.4 | async-start | bytes 8388608
  397.2 12.7 %slice-start.8 = ((s8[4718592]{0:T(1024)(128)(4,1)}), s8[4194304]{0:T(1024)(128)(4,1)S(1)}, s32[]{:S(2)}) async-start(s8[4718592]{0:T(1024)(128)(4,1)} %bitcast.223), calls=%async_computation.12 | async-start | bytes 8388608
  399.6 10.3 %slice-start.1 = ((s8[4718592]{0:T(1024)(128)(4,1)}), s8[524288]{0:T(1024)(128)(4,1)S(1)}, s32[]{:S(2)}) async-start(s8[4718592]{0:T(1024)(128)(4,1)} %bitcast.201), calls=%async_computation.5 | async-start | bytes 1048576
  399.6 10.3 %copy-start.35 = (f32[1536]{0:T(1024)S(1)}, f32[1536]{0:T(1024)}, u32[]{:S(2)}) copy-start(f32[1536]{0:T(1024)} %copy-done.34) | copy-start | bytes 18436
  399.6 10.3 %copy-start.37 = (f32[1536]{0:T(1024)S(1)}, f32[1536]{0:T(1024)}, u32[]{:S(2)}) copy-start(f32[1536]{0:T(1024)} %copy-done.36) | copy-start | bytes 18436
  399.6 10.3 %copy-start.42 = (f32[768]{0:T(1024)S(1)}, f32[768]{0:T(1024)}, u32[]{:S(2)}) copy-start(f32[768]{0:T(1024)} %param.34) | copy-start | bytes 9220
  399.6 10.3 %copy-start.60 = (f32[768]{0:T(1024)S(1)}, f32[768]{0:T(1024)}, u32[]{:S(2)}) copy-start(f32[768]{0:T(1024)} %param.35) | copy-start | bytes 9220
  399.6 10.3 %slice-start.9 = ((s8[4718592]{0:T(1024)(128)(4,1)}), s8[524288]{0:T(1024)(128)(4,1)S(1)}, s32[]{:S(2)}) async-start(s8[4718592]{0:T(1024)(128)(4,1)} %bitcast.223), calls=%async_computation.13 | async-start | bytes 1048576
  410.0 6.0 copy-start.10
  416.0 7.3 slice-start.2
  418.4 4.9 slice-start.3
  418.4 4.9 copy-start.12
  425.4 12.3 %copy-start.39 = (f32[768]{0:T(1024)S(1)}, f32[768]{0:T(1024)}, u32[]{:S(2)}) copy-start(f32[768]{0:T(1024)} %param.25) | copy-start | bytes 9220
  425.4 16.3 %copy-start.43 = (f32[768]{0:T(1024)S(1)}, f32[768]{0:T(1024)}, u32[]{:S(2)}) copy-start(f32[768]{0:T(1024)} %get-tuple-element.211) | copy-start | bytes 9220
  425.4 16.3 %copy-start.44 = (f32[768]{0:T(1024)S(1)}, f32[768]{0:T(1024)}, u32[]{:S(2)}) copy-start(f32[768]{0:T(1024)} %get-tuple-element.217) | copy-start | bytes 9220
  425.5 16.3 %copy-start.46 = (f32[768]{0:T(1024)S(1)}, f32[768]{0:T(1024)}, u32[]{:S(2)}) copy-start(f32[768]{0:T(1024)} %get-tuple-element.272) | copy-start | bytes 9220
  425.5 16.3 %copy-start.47 = (f32[768]{0:T(1024)S(1)}, f32[768]{0:T(1024)}, u32[]{:S(2)}) copy-start(f32[768]{0:T(1024)} %get-tuple-element.278) | copy-start | bytes 9220
  425.5 16.3 %copy-start.53 = (f32[1536]{0:T(1024)S(1)}, f32[1536]{0:T(1024)}, u32[]{:S(2)}) copy-start(f32[1536]{0:T(1024)} %get-tuple-element.285) | copy-start | bytes 18436
  425.5 98.5 %copy-start.55 = (f32[768]{0:T(1024)S(1)}, f32[768]{0:T(1024)}, u32[]{:S(2)}) copy-start(f32[768]{0:T(1024)} %param.39) | copy-start | bytes 9220
  437.7 92.7 %slice-start.4 = ((s8[4718592]{0:T(1024)(128)(4,1)}), s8[524288]{0:T(1024)(128)(4,1)S(1)}, s32[]{:S(2)}) async-start(s8[4718592]{0:T(1024)(128)(4,1)} %bitcast.205), calls=%async_computation.8 | async-start | bytes 1048576
  524.0 6.4 slice-start.5
  524.0 7.9 copy-start.8
  847.2 5.2 copy-start.22
  847.2 6.2 copy-start.21
  847.2 7.2 copy-start.13
  853.4 4.2 slice-start.6
  854.4 5.7 copy-start.1
  (25 other events, 44.0 us)
Sparse Core Ops, SparseCore 0:
  130.8 31.8 all-reduce.7
  189.0 30.3 all-reduce.9
  395.7 41.9 all-reduce.13
  445.1 401.9 all-reduce.11
where the time goes:
time: 878 us; the launch traced here: 867 us
  waiting for transfers between devices  373 us (42%)
  matrix products  256 us (29%)
  other arithmetic  87.6 us (10%)
  blocking collectives  82.2 us (9%)
  local copies, waits for them, and re-layouts  52 us (6%)
  between operations  15.7 us (2%)
    psum x1, waiting for transfers between devices, on_device(): lax.psum((g_norm1_gain, g_norm1_bias, g_query_w, g_query_b, g_key_w, g_va...  312 us
    dot_general x21, matrix products, contract(): return jnp.einsum(form, left, right, preferred_element_type=jnp.float32)  182 us
    psum x1, blocking collectives, on_device(): lax.psum((g_norm1_gain, g_norm1_bias, g_query_w, g_query_b, g_key_w, g_va...  82.2 us
    dot_general x18, matrix products, mat_dot(): return jnp.dot(left, right, preferred_element_type=jnp.float32)  74.1 us
    unnamed x150, local copies, waits for them, and re-layouts  31.7 us
    psum x1, waiting for transfers between devices, on_device(): attn_total = lax.psum(mat_dot(attended_flat, output_weight), 'tensor')  30.7 us
    reduce_sum x3, other arithmetic, per_block(): totals = jnp.sum(exponent, axis=-1, keepdims=True)  30.6 us
    psum x1, waiting for transfers between devices, on_device(): grad_two = lax.psum(mat_dot(grad_pre_b, hidden_weight.T), 'tensor')  18.3 us
  transfers between devices with their start and end apart: 4, of which 4 were waited for; matrix products, arithmetic and copies ran while one was open for 6% of the time, Pallas kernels for 0%

commit v1 on v0

--- a/solution.py
+++ b/solution.py
@@ -1,8 +1,11 @@
+import functools
 import math
 
 import jax
 import jax.numpy as jnp
 from jax import lax
+from jax.experimental import pallas as pl
+from jax.experimental.pallas import tpu as pltpu
 from jax.sharding import PartitionSpec as P
 
 HD = 64
@@ -101,7 +104,212 @@
     return (grad_query.reshape(total_rows, head_count, head_size), grad_keys, grad_values)
 
 
+MESH_ID = pl.DeviceIdType.MESH
+
+
+def bit_of(index, bit):
+    return (index // bit) % 2
+
+
+def partner_of(index, bit):
+    return index + bit - 2 * bit * bit_of(index, bit)
+
+
+class Unit:
+    def __init__(self, buffer, total, place, order, extra, landing, sems, me, core):
+        row, rows, col, cols = place
+        send_sem, recv_sems, own_sem = sems
+        self.buffer, self.total, self.landing = buffer, total, landing
+        self.columns = pl.ds(col, cols)
+        self.rows = rows
+        self.order, self.extra = order, extra
+        self.send_sem, self.recv_sems, self.own_sem = send_sem, recv_sems, own_sem
+        self.me, self.core = me, core
+        self.last = None
+        self.offsets = [row]
+        self.lands = [0]
+        for step, bit in enumerate(order):
+            self.offsets.append(self.offsets[-1] + bit_of(me, bit) * (rows >> (step + 1)))
+            self.lands.append(self.lands[-1] + (rows >> (step + 1)))
+        self.stages = 2 * len(order) + len(extra)
+
+    def part(self, array, offset, length):
+        return array.at[pl.ds(pl.multiple_of(offset, 8), length), self.columns]
+
+    def own_copy(self):
+        length = self.rows >> len(self.order)
+        return pltpu.make_async_copy(
+            self.part(self.buffer, self.offsets[-1], length),
+            self.part(self.total, self.offsets[-1], length),
+            self.own_sem,
+        )
+
+    def copy(self, stage):
+        halvings = len(self.order)
+        doublings = len(self.extra)
+        if stage < halvings:
+            bit = self.order[stage]
+            length = self.rows >> (stage + 1)
+            source = self.part(self.buffer, self.offsets[stage] + (1 - bit_of(self.me, bit)) * length, length)
+            target = self.landing.at[pl.ds(self.lands[stage], length), :]
+        elif stage < halvings + doublings:
+            bit = self.extra[stage - halvings]
+            length = self.rows >> halvings
+            source = self.part(self.buffer, self.offsets[-1], length)
+            target = self.landing.at[pl.ds(self.lands[-1] + (stage - halvings) * length, length), :]
+        else:
+            step = 2 * halvings + doublings - 1 - stage
+            bit = self.order[step]
+            length = self.rows >> (step + 1)
+            target = self.part(self.total, self.offsets[step + 1], length)
+            source = target
+            if step == halvings - 1:
+                source = self.part(self.buffer, self.offsets[step + 1], length)
+        return pltpu.make_async_remote_copy(
+            src_ref=source,
+            dst_ref=target,
+            send_sem=self.send_sem,
+            recv_sem=self.recv_sems.at[stage],
+            device_id=(partner_of(self.me, bit), self.core),
+            device_id_type=MESH_ID,
+        )
+
+    def advance(self, stage):
+        halvings = len(self.order)
+        doublings = len(self.extra)
+        if stage > 0:
+            self.last.wait()
+            if stage <= halvings + doublings:
+                step = min(stage, halvings)
+                length = self.rows >> step
+                if stage <= halvings:
+                    land = self.lands[stage - 1]
+                else:
+                    land = self.lands[-1] + (stage - 1 - halvings) * length
+                index = (pl.ds(pl.multiple_of(self.offsets[step], 8), length), self.columns)
+                self.buffer[index] = self.buffer[index] + self.landing[pl.ds(land, length), :]
+            if stage == halvings + doublings:
+                self.own_copy().start()
+            if stage == halvings + doublings + 1:
+                self.own_copy().wait()
+        if stage < self.stages:
+            self.last = self.copy(stage)
+            self.last.start()
+
+
+def dp_bits(size):
+    return [1 << power for power in range(size.bit_length() - 1)]
+
+
+def orders_of(size):
+    bits = dp_bits(size)
+    a, b, c, d = bits[:4]
+    return [[a, b, c, d], [b, a, c, d], [c, a, b, d], [c, b, a, d]], bits[4:]
+
+
+def landing_rows(rows, extra):
+    return rows - (rows >> 4) + len(extra) * (rows >> 4)
+
+
+def gradient_places():
+    waves = []
+    for j in range(3):
+        waves.append([(4, (512 * j, 512, 256 * c, 256), 0) for c in range(3)])
+        waves.append([(5, (256 * c, 256, 512 * j, 512), 1) for c in range(3)])
+    for j in range(3):
+        waves.append([(j, (256 * c, 256, 0, 384), 2) for c in range(3)])
+    waves.append([(3, (0, 384, 256 * c, 256), 3) for c in range(3)])
+    return waves
+
+
+def sum_kernel(size, *refs):
+    sources, totals = refs[:7], refs[7:14]
+    landings, (send_sems, recv_sems, own_sems) = refs[14:19], refs[19:22]
+    held = refs[22:]
+    me, core = lax.axis_index("dp"), lax.axis_index("tensor")
+    barrier = pltpu.get_barrier_semaphore()
+    bits = dp_bits(size)
+    for bit in bits:
+        pl.semaphore_signal(
+            barrier, inc=1, device_id=(partner_of(me, bit), core), device_id_type=MESH_ID
+        )
+    pl.semaphore_wait(barrier, len(bits))
+    orders, spare = orders_of(size)
+    for at, source in enumerate(sources):
+        pltpu.make_async_copy(source, held[at], own_sems.at[at]).start()
+    for at, source in enumerate(sources):
+        pltpu.make_async_copy(source, held[at], own_sems.at[at]).wait()
+    used = [0] * 5
+    waves = []
+    number = 0
+    for at, places in enumerate(gradient_places() + [[(6, (0, 128, 0, 128), 4)]]):
+        wave = []
+        for kind, (which, place, shelf) in enumerate(places):
+            order = orders[kind] if kind < 2 else orders[2 + at % 2]
+            landing = landings[shelf].at[used[shelf]]
+            used[shelf] += 1
+            wave.append(
+                Unit(
+                    held[which], totals[which], place, order, spare, landing,
+                    (send_sems.at[number], recv_sems.at[number], own_sems.at[number]), me, core,
+                )
+            )
+            number += 1
+        waves.append(wave)
+    last = waves[0][0].stages
+    for tick in range(len(waves) + last):
+        for at, wave in enumerate(waves):
+            if 0 <= tick - at <= last:
+                for unit in wave:
+                    unit.advance(tick - at)
+
+
+def sum_over_dp(size, arrays):
+    spare = orders_of(size)[1]
+    stages = 8 + len(spare)
+    shelves = [(9, 512, 256), (9, 256, 512), (9, 256, 384), (3, 384, 256), (1, 128, 128)]
+    return pl.pallas_call(
+        functools.partial(sum_kernel, size),
+        out_shape=[jax.ShapeDtypeStruct(array.shape, jnp.float32) for array in arrays],
+        in_specs=[pl.BlockSpec(memory_space=pl.ANY)] * 7,
+        out_specs=[pl.BlockSpec(memory_space=pl.ANY)] * 7,
+        scratch_shapes=[
+            pltpu.VMEM((count, landing_rows(rows, spare), cols), jnp.float32)
+            for count, rows, cols in shelves
+        ]
+        + [
+            pltpu.SemaphoreType.DMA((31,)),
+            pltpu.SemaphoreType.DMA((31, stages)),
+            pltpu.SemaphoreType.DMA((31,)),
+        ]
+        + [pltpu.VMEM(array.shape, jnp.float32) for array in arrays],
+        compiler_params=pltpu.CompilerParams(
+            collective_id=0, has_side_effects=True, vmem_limit_bytes=60 * 2**20
+        ),
+        name="sum_over_dp",
+    )(*arrays)
+
+
+SMALL_ROWS, SMALL_COLS = 128, 128
+
+
+def pack_small(vectors):
+    flat = jnp.concatenate(vectors)
+    flat = jnp.pad(flat, (0, SMALL_ROWS * SMALL_COLS - flat.shape[0]))
+    return flat.reshape(SMALL_ROWS, SMALL_COLS)
+
+
+def unpack_small(packed, vectors):
+    flat = packed.reshape(-1)
+    out, at = [], 0
+    for vector in vectors:
+        out.append(lax.slice(flat, (at,), (at + vector.shape[0],)))
+        at += vector.shape[0]
+    return out
+
+
 def on_device(
+    size,
     frames,
     lengths,
     cotangent,
@@ -196,43 +404,18 @@
     input_grad = (grad_resid + norm_back(grad_one, unit_one, inverse_one, norm1_gain)).astype(
         jnp.bfloat16
     )
-    summed = lax.psum(
-        (
-            g_norm1_gain,
-            g_norm1_bias,
-            g_query_w,
-            g_query_b,
-            g_key_w,
-            g_value_w,
-            g_value_b,
-            g_output_w,
-            g_output_b,
-            g_norm2_gain,
-            g_norm2_bias,
-            g_hidden_w,
-            g_hidden_b,
-            g_proj_w,
-            g_proj_b,
-        ),
-        "dp",
-    )
+    small = [
+        g_norm1_gain, g_norm1_bias, g_query_b, g_value_b, g_output_b,
+        g_norm2_gain, g_norm2_bias, g_hidden_b, g_proj_b,
+    ]
+    summed = sum_over_dp(
+        size, [g_query_w, g_key_w, g_value_w, g_output_w, g_proj_w, g_hidden_w, pack_small(small)]
+    )
+    s_query_w, s_key_w, s_value_w, s_output_w, s_proj_w, s_hidden_w, packed = summed
     (
-        s_norm1_gain,
-        s_norm1_bias,
-        s_query_w,
-        s_query_b,
-        s_key_w,
-        s_value_w,
-        s_value_b,
-        s_output_w,
-        s_output_b,
-        s_norm2_gain,
-        s_norm2_bias,
-        s_hidden_w,
-        s_hidden_b,
-        s_proj_w,
-        s_proj_b,
-    ) = summed
+        s_norm1_gain, s_norm1_bias, s_query_b, s_value_b, s_output_b,
+        s_norm2_gain, s_norm2_bias, s_hidden_b, s_proj_b,
+    ) = unpack_small(packed, small)
     return (
         block_out[None],
         input_grad[None],
@@ -276,7 +459,7 @@
         P(),
     )
     return jax.shard_map(
-        on_device,
+        functools.partial(on_device, mesh.shape["dp"]),
         mesh=mesh,
         in_specs=placed,
         out_specs=(

time: 878 us -> 706 us (0.80)
  waiting for transfers between devices: 373 us -> 52.3 us
  Pallas kernels: 0 us -> 222 us
  blocking collectives: 82.2 us -> 0 us
    psum x1 -> x0, waiting for transfers between devices: 312 us -> none  [on_device(): lax.psum((g_norm1_gain, g_norm1_bias, g_query_w, g_query_b, g_key_w, g_va...]
    pallas_call x0 -> x1, Pallas kernels: none -> 222 us  [sum_over_dp(): pl.pallas_call(functools.partial(sum_kernel, size), out_shape=[jax.ShapeD...]
    psum x1 -> x0, blocking collectives: 82.2 us -> none  [on_device(): lax.psum((g_norm1_gain, g_norm1_bias, g_query_w, g_query_b, g_key_w, g_va...]
    unnamed x150 -> x164, local copies, waits for them, and re-layouts: 31.7 us -> 27 us
  transfers between devices with their start and end apart: 4 -> 3, of which waited for: 4 -> 3; matrix products, arithmetic and copies ran while one was open for 6% -> 7% of each run, Pallas kernels for 0% -> 0%
where the time goes in v1:
time: 706 us; the launch traced here: 695 us
  matrix products  261 us (37%)
  Pallas kernels  222 us (31%)
  other arithmetic  89 us (13%)
  local copies, waits for them, and re-layouts  54.5 us (8%)
  waiting for transfers between devices  52.3 us (7%)
  between operations  15.5 us (2%)
    pallas_call x1, Pallas kernels, sum_over_dp(): pl.pallas_call(functools.partial(sum_kernel, size), out_shape=[jax.ShapeD...  222 us
    dot_general x21, matrix products, contract(): return jnp.einsum(form, left, right, preferred_element_type=jnp.float32)  181 us
    dot_general x18, matrix products, mat_dot(): return jnp.dot(left, right, preferred_element_type=jnp.float32)  79.7 us
    psum x1, waiting for transfers between devices, on_device(): attn_total = lax.psum(mat_dot(attended_flat, output_weight), 'tensor')  30.7 us
    reduce_sum x3, other arithmetic, per_block(): totals = jnp.sum(exponent, axis=-1, keepdims=True)  30.6 us
    unnamed x164, local copies, waits for them, and re-layouts  27 us
    psum x1, waiting for transfers between devices, on_device(): grad_two = lax.psum(mat_dot(grad_pre_b, hidden_weight.T), 'tensor')  18.3 us
  transfers between devices with their start and end apart: 3, of which 3 were waited for; matrix products, arithmetic and copies ran while one was open for 7% of the time, Pallas kernels for 0%

profile of v1, /device:TPU:0, one launch (start us, length us, event | category | flops | bytes accessed | tf_op | source)
XLA Modules:
  0.0 695.2 jit_solution(621989719352617577)
XLA Ops:
  7.3 2.2 convert_reduce_fusion
  9.5 2.5 fusion.63
  16.7 3.1 reshape.237
  19.8 4.4 copy.39
  24.2 2.9 convolution_convert_fusion.1
  27.1 3.9 fusion.71
  31.1 92.4 %while.28 = (s32[]{:T(128)}, bf16[3,512,6,64]{1,3,2,0:T(8,128)(2,1)}, f32[3,6,512]{2,1,0:T(8,128)}, bf16[3,512,6,64]{1,3,2,0:T(8,128)(2,1)}, bf16[1536,6,64]{0,2...) while((s32[]{:T(128)}, bf16[3,512,6,64]{1,3,2,0:T(8,128)(2,1)}, ...), condition=%wide.region_5.6_spmd.clone, body=%wide.region_2.5_spmd.clone.sunk | while | flops 1250621952 | bytes 59893876 | solution.py:66
  31.7 9.1 %select_reduce_fusion.2 = (f32[6,512]{1,0:T(8,128)S(1)}, f32[6,512,1536]{2,1,0:T(8,128)}) fusion(pred[1536]{0:T(1024)(128)(4,1)S(1)} %iota_compare_fusion.5, bf16[1536,6,64]{0,2,1:T(8,128)(2,1)S(1)} %get-tuple-element.432, bf16[3,512,6,64]{1,3,2,0:T(8,128)(2,1)} %get-tuple-element.431, s32[]{:T(128)} %get-tuple-element.420), kind=kOutput, calls=%fused_computation.4.clone.1 | convolution fusion | flops 613413888 | bytes 20461568 | tf_op jit(solution)/shard_map/while/body/eval_jaxpr/qhd,khd->hqk/dot_general | solution.py:20
  40.8 10.2 %fusion.154 = f32[6,512]{1,0:T(8,128)} fusion(f32[6,512,1536]{2,1,0:T(8,128)} %get-tuple-element.399, f32[6,512]{1,0:T(8,128)S(1)} %get-tuple-element.400, pred[1536]{0:T(1024)(128)(4,1)} %copy-done.23), kind=kLoop, calls=%fused_computation.5.clone.1 | loop fusion | flops 14152704 | bytes 18900480 | tf_op jit(solution)/shard_map/while/body/eval_jaxpr/reduce_sum | solution.py:61
  52.3 9.5 %fusion.155 = bf16[3,512,6,64]{1,3,2,0:T(8,128)(2,1)} fusion(bf16[3,512,6,64]{1,3,2,0:T(8,128)(2,1)} %get-tuple-element.421, s32[]{:T(128)} %get-tuple-element.420, bf16[1536,6,64]{0,2,1:T(8,128)(2,1)} %get-tuple-element.433, f32[6,512,1536]{2,1,0:T(8,128)} %get-tuple-element.399, f32[6,512]{1,0:T(8,128)} %fusion.154, ...), kind=kOutput, calls=%fused_computation.9.clone.1 | convolution fusion | flops 623050752 | bytes 20478464 | tf_op jit(solution)/shard_map/while/body/eval_jaxpr/hqk,khd->qhd/dot_general | solution.py:20
  62.5 9.1 %select_reduce_fusion.2 = (f32[6,512]{1,0:T(8,128)S(1)}, f32[6,512,1536]{2,1,0:T(8,128)}) fusion(pred[1536]{0:T(1024)(128)(4,1)S(1)} %iota_compare_fusion.5, bf16[1536,6,64]{0,2,1:T(8,128)(2,1)S(1)} %get-tuple-element.432, bf16[3,512,6,64]{1,3,2,0:T(8,128)(2,1)} %get-tuple-element.431, s32[]{:T(128)} %get-tuple-element.420), kind=kOutput, calls=%fused_computation.4.clone.1 | convolution fusion | flops 613413888 | bytes 20461568 | tf_op jit(solution)/shard_map/while/body/eval_jaxpr/qhd,khd->hqk/dot_general | solution.py:20
  71.6 10.2 %fusion.154 = f32[6,512]{1,0:T(8,128)} fusion(f32[6,512,1536]{2,1,0:T(8,128)} %get-tuple-element.399, f32[6,512]{1,0:T(8,128)S(1)} %get-tuple-element.400, pred[1536]{0:T(1024)(128)(4,1)} %copy-done.23), kind=kLoop, calls=%fused_computation.5.clone.1 | loop fusion | flops 14152704 | bytes 18900480 | tf_op jit(solution)/shard_map/while/body/eval_jaxpr/reduce_sum | solution.py:61
  83.1 9.5 %fusion.155 = bf16[3,512,6,64]{1,3,2,0:T(8,128)(2,1)} fusion(bf16[3,512,6,64]{1,3,2,0:T(8,128)(2,1)} %get-tuple-element.421, s32[]{:T(128)} %get-tuple-element.420, bf16[1536,6,64]{0,2,1:T(8,128)(2,1)} %get-tuple-element.433, f32[6,512,1536]{2,1,0:T(8,128)} %get-tuple-element.399, f32[6,512]{1,0:T(8,128)} %fusion.154, ...), kind=kOutput, calls=%fused_computation.9.clone.1 | convolution fusion | flops 623050752 | bytes 20478464 | tf_op jit(solution)/shard_map/while/body/eval_jaxpr/hqk,khd->qhd/dot_general | solution.py:20
  93.2 9.1 %select_reduce_fusion.2 = (f32[6,512]{1,0:T(8,128)S(1)}, f32[6,512,1536]{2,1,0:T(8,128)}) fusion(pred[1536]{0:T(1024)(128)(4,1)S(1)} %iota_compare_fusion.5, bf16[1536,6,64]{0,2,1:T(8,128)(2,1)S(1)} %get-tuple-element.432, bf16[3,512,6,64]{1,3,2,0:T(8,128)(2,1)} %get-tuple-element.431, s32[]{:T(128)} %get-tuple-element.420), kind=kOutput, calls=%fused_computation.4.clone.1 | convolution fusion | flops 613413888 | bytes 20461568 | tf_op jit(solution)/shard_map/while/body/eval_jaxpr/qhd,khd->hqk/dot_general | solution.py:20
  102.3 10.2 %fusion.154 = f32[6,512]{1,0:T(8,128)} fusion(f32[6,512,1536]{2,1,0:T(8,128)} %get-tuple-element.399, f32[6,512]{1,0:T(8,128)S(1)} %get-tuple-element.400, pred[1536]{0:T(1024)(128)(4,1)} %copy-done.23), kind=kLoop, calls=%fused_computation.5.clone.1 | loop fusion | flops 14152704 | bytes 18900480 | tf_op jit(solution)/shard_map/while/body/eval_jaxpr/reduce_sum | solution.py:61
  113.8 9.5 %fusion.155 = bf16[3,512,6,64]{1,3,2,0:T(8,128)(2,1)} fusion(bf16[3,512,6,64]{1,3,2,0:T(8,128)(2,1)} %get-tuple-element.421, s32[]{:T(128)} %get-tuple-element.420, bf16[1536,6,64]{0,2,1:T(8,128)(2,1)} %get-tuple-element.433, f32[6,512,1536]{2,1,0:T(8,128)} %get-tuple-element.399, f32[6,512]{1,0:T(8,128)} %fusion.154, ...), kind=kOutput, calls=%fused_computation.9.clone.1 | convolution fusion | flops 623050752 | bytes 20478464 | tf_op jit(solution)/shard_map/while/body/eval_jaxpr/hqk,khd->qhd/dot_general | solution.py:20
  123.5 2.3 copy.40
  127.3 3.6 fusion.90
  132.2 30.7 %all-reduce.6.cloned.1.call-done = f32[1536,768]{1,0:T(8,128)} async-done(((f32[1536,768]{1,0:T(8,128)}), f32[1536,768]{1,0:T(8,128)}) %all-reduce.6.cloned.1.call-update) | async-done | bytes 4718608 | tf_op jit(solution)/shard_map/psum | solution.py:349
  162.9 3.8 fusion.85
  167.6 6.4 multiply_convert_fusion.1
  174.0 7.4 %fusion.89 = (f32[1536]{0:T(1024)}, bf16[1536,1536]{1,0:T(8,128)(2,1)S(1)}) fusion(f32[1536,1536]{1,0:T(8,128)S(1)} %get-tuple-element.291, bf16[1536,768]{1,0:T(8,128)(2,1)S(1)} %copy-done.57, bf16[1,1536,768]{2,1,0:T(8,128)(2,1)S(1)} %copy-done.13, pred[1536]{0:T(1024)(128)(4,1)S(1)} %copy-done.49), kind=kOutput, calls=%fused_computation.147 | convolution fusion | flops 3651009024 | bytes 18882048 | tf_op jit(solution)/shard_map/dot_general | solution.py:24
  181.4 2.2 copy-done.65
  183.6 5.5 fusion.78
  192.6 8.7 %fusion.91 = f32[1536,768]{1,0:T(8,128)} fusion(bf16[1536,1536]{1,0:T(8,128)(2,1)} %get-tuple-element.290, bf16[1536,768]{1,0:T(8,128)(2,1)S(1)} %copy-done.58), kind=kOutput, calls=%fused_computation.149 | convolution fusion | flops 3623878656 | bytes 11796480 | tf_op jit(solution)/shard_map/dot_general | solution.py:24
  201.3 18.3 %all-reduce.8.cloned.1.call-done = f32[1536,768]{1,0:T(8,128)} async-done(((f32[1536,768]{1,0:T(8,128)}), f32[1536,768]{1,0:T(8,128)}) %all-reduce.8.cloned.1.call-update) | async-done | bytes 4718608 | tf_op jit(solution)/shard_map/psum | solution.py:368
  219.7 5.8 multiply_reduce_fusion
  225.5 5.1 fusion.84
  232.8 2.1 convolution_convert_fusion
  234.9 3.9 reshape_reshape.13
  238.8 2.7 copy.43
  241.5 3.0 fusion.75
  244.4 136.3 %while.29 = (s32[]{:T(128)}, f32[1536,6,64]{0,2,1:T(8,128)S(1)}, f32[1536,6,64]{0,2,1:T(8,128)}, f32[3,512,6,64]{1,3,2,0:T(8,128)}, bf16[3,512,6,64]{1,3,2,0:T(8...) while((s32[]{:T(128)}, f32[1536,6,64]{0,2,1:T(8,128)S(1)}, ...), condition=%wide.region_15.16_spmd.clone, body=%wide.region_14.15_spmd.clone.sunk | while | flops 3060205056 | bytes 142843152 | solution.py:94
  244.4 9.2 %fusion.166 = f32[6,512,1536]{2,1,0:T(8,128)} fusion(bf16[1536,6,64]{0,2,1:T(8,128)(2,1)S(1)} %get-tuple-element.467, bf16[3,512,6,64]{1,3,2,0:T(8,128)(2,1)} %get-tuple-element.466, s32[]{:T(128)} %get-tuple-element.449), kind=kOutput, calls=%fused_computation.34.clone.1 | convolution fusion | flops 603979776 | bytes 20447744 | tf_op jit(solution)/shard_map/while/body/eval_jaxpr/qhd,khd->hqk/dot_general | solution.py:20
  256.3 11.2 %multiply_convert_fusion.3 = bf16[6,512,1536]{2,1,0:T(8,128)(2,1)} fusion(f32[6,512,1536]{2,1,0:T(8,128)} %fusion.166, f32[6,512]{1,0:T(8,128)S(1)} %dynamic-slice_bitcast_fusion.4, f32[6,512]{1,0:T(8,128)S(1)} %dynamic-slice_bitcast_fusion.5, pred[1536]{0:T(1024)(128)(4,1)S(1)} %iota_compare_fusion.6, bf16[1536,6,64]{0,2,1:T(8,128)(2,1)S(1)} %copy-done.64, ...), kind=kOutput, calls=%fused_computation.17.clone.1 | convolution fusion | flops 627572736 | bytes 29911040 | tf_op jit(solution)/shard_map/while/body/eval_jaxpr/qhd,khd->hqk/dot_general | solution.py:20
  267.5 5.8 fusion.167
  274.0 3.9 fusion.169
  277.8 11.4 %fusion.168 = f32[1536,6,64]{0,2,1:T(8,128)} fusion(f32[6,512,1536]{2,1,0:T(8,128)} %fusion.166, f32[6,512]{1,0:T(8,128)S(1)} %dynamic-slice_bitcast_fusion.5, pred[1536]{0:T(1024)(128)(4,1)S(1)} %copy-done.31, f32[1536,6,64]{0,2,1:T(8,128)} %get-tuple-element.451, pred[]{:T(512)S(6)} %compare.4, bf16[3,512,6,64]{1,3,2,0:T(8,128)(2,1)} %get-tuple-element.469, ...), kind=kOutput, calls=%fused_computation.25.clone.1 | convolution fusion | flops 619315200 | bytes 24000512 | tf_op jit(solution)/shard_map/while/body/eval_jaxpr/hqk,qhd->khd/dot_general | solution.py:20
  289.3 9.2 %fusion.166 = f32[6,512,1536]{2,1,0:T(8,128)} fusion(bf16[1536,6,64]{0,2,1:T(8,128)(2,1)S(1)} %get-tuple-element.467, bf16[3,512,6,64]{1,3,2,0:T(8,128)(2,1)} %get-tuple-element.466, s32[]{:T(128)} %get-tuple-element.449), kind=kOutput, calls=%fused_computation.34.clone.1 | convolution fusion | flops 603979776 | bytes 20447744 | tf_op jit(solution)/shard_map/while/body/eval_jaxpr/qhd,khd->hqk/dot_general | solution.py:20
  301.1 11.2 %multiply_convert_fusion.3 = bf16[6,512,1536]{2,1,0:T(8,128)(2,1)} fusion(f32[6,512,1536]{2,1,0:T(8,128)} %fusion.166, f32[6,512]{1,0:T(8,128)S(1)} %dynamic-slice_bitcast_fusion.4, f32[6,512]{1,0:T(8,128)S(1)} %dynamic-slice_bitcast_fusion.5, pred[1536]{0:T(1024)(128)(4,1)S(1)} %iota_compare_fusion.6, bf16[1536,6,64]{0,2,1:T(8,128)(2,1)S(1)} %copy-done.64, ...), kind=kOutput, calls=%fused_computation.17.clone.1 | convolution fusion | flops 627572736 | bytes 29911040 | tf_op jit(solution)/shard_map/while/body/eval_jaxpr/qhd,khd->hqk/dot_general | solution.py:20
  312.3 5.8 fusion.167
  318.8 3.9 fusion.169
  322.7 12.1 %fusion.168 = f32[1536,6,64]{0,2,1:T(8,128)} fusion(f32[6,512,1536]{2,1,0:T(8,128)} %fusion.166, f32[6,512]{1,0:T(8,128)S(1)} %dynamic-slice_bitcast_fusion.5, pred[1536]{0:T(1024)(128)(4,1)S(1)} %copy-done.31, f32[1536,6,64]{0,2,1:T(8,128)} %get-tuple-element.451, pred[]{:T(512)S(6)} %compare.4, bf16[3,512,6,64]{1,3,2,0:T(8,128)(2,1)} %get-tuple-element.469, ...), kind=kOutput, calls=%fused_computation.25.clone.1 | convolution fusion | flops 619315200 | bytes 24000512 | tf_op jit(solution)/shard_map/while/body/eval_jaxpr/hqk,qhd->khd/dot_general | solution.py:20
  334.8 9.2 %fusion.166 = f32[6,512,1536]{2,1,0:T(8,128)} fusion(bf16[1536,6,64]{0,2,1:T(8,128)(2,1)S(1)} %get-tuple-element.467, bf16[3,512,6,64]{1,3,2,0:T(8,128)(2,1)} %get-tuple-element.466, s32[]{:T(128)} %get-tuple-element.449), kind=kOutput, calls=%fused_computation.34.clone.1 | convolution fusion | flops 603979776 | bytes 20447744 | tf_op jit(solution)/shard_map/while/body/eval_jaxpr/qhd,khd->hqk/dot_general | solution.py:20
  346.6 11.2 %multiply_convert_fusion.3 = bf16[6,512,1536]{2,1,0:T(8,128)(2,1)} fusion(f32[6,512,1536]{2,1,0:T(8,128)} %fusion.166, f32[6,512]{1,0:T(8,128)S(1)} %dynamic-slice_bitcast_fusion.4, f32[6,512]{1,0:T(8,128)S(1)} %dynamic-slice_bitcast_fusion.5, pred[1536]{0:T(1024)(128)(4,1)S(1)} %iota_compare_fusion.6, bf16[1536,6,64]{0,2,1:T(8,128)(2,1)S(1)} %copy-done.64, ...), kind=kOutput, calls=%fused_computation.17.clone.1 | convolution fusion | flops 627572736 | bytes 29911040 | tf_op jit(solution)/shard_map/while/body/eval_jaxpr/qhd,khd->hqk/dot_general | solution.py:20
  357.8 5.8 fusion.167
  364.3 3.9 fusion.169
  368.2 12.1 %fusion.168 = f32[1536,6,64]{0,2,1:T(8,128)} fusion(f32[6,512,1536]{2,1,0:T(8,128)} %fusion.166, f32[6,512]{1,0:T(8,128)S(1)} %dynamic-slice_bitcast_fusion.5, pred[1536]{0:T(1024)(128)(4,1)S(1)} %copy-done.31, f32[1536,6,64]{0,2,1:T(8,128)} %get-tuple-element.451, pred[]{:T(512)S(6)} %compare.4, bf16[3,512,6,64]{1,3,2,0:T(8,128)(2,1)} %get-tuple-element.469, ...), kind=kOutput, calls=%fused_computation.25.clone.1 | convolution fusion | flops 619315200 | bytes 24000512 | tf_op jit(solution)/shard_map/while/body/eval_jaxpr/hqk,qhd->khd/dot_general | solution.py:20
  380.7 3.3 fusion.88
  388.5 3.2 fusion.87
  391.7 3.6 add_add_fusion
  397.0 3.0 fusion.73
  400.1 11.2 %fusion.83.refs_4_ = f32[1536,768]{1,0:T(8,128)} fusion(bf16[1536,1536]{1,0:T(8,128)(2,1)} %get-tuple-element.290, bf16[1,1536,768]{2,1,0:T(8,128)(2,1)} %param.24, pred[1536]{0:T(1024)(128)(4,1)S(1)} %copy-done.51), kind=kOutput, calls=%fused_computation.142 | convolution fusion | flops 3625058304 | bytes 11798016 | tf_op jit(solution)/shard_map/dot_general | solution.py:24
  411.4 6.2 fusion.76.refs_5_
  420.2 4.9 fusion.94.refs_0_
  425.1 4.5 fusion.96.refs_2_
  429.6 2.4 fusion.95.refs_1_
  434.2 3.2 all-reduce.10.cloned.1.call-done
  437.4 3.9 fusion.62
  442.2 221.9 %sum_over_dp.1 = (f32[768,384]{1,0:T(8,128)}, f32[768,384]{1,0:T(8,128)}, f32[768,384]{1,0:T(8,128)}, f32[384,768]{1,0:T(8,128)}, f32[1536,768]{1,0:T(8,128)}, /*index=5*/f32[768,1536]{1,0:T(8,128)}, f32[128,128]{1,0:T(8,128)}) custom-call(f32[768,384]{1,0:T(8,128)} %fusion.94.refs_0_, f32[768,384]{1,0:T(8,128)} %fusion.95.refs_1_, ...), custom_call_target="tpu_custom_call" | custom-call | tf_op jit(solution)/shard_map/sum_over_dp/pallas_call | solution.py:271
  668.3 5.8 fusion.74
  674.1 4.6 fusion.72
  682.8 2.4 copy.98
  686.3 2.2 copy.99
  (247 shorter events, 50.1 us)
Async XLA Ops:
  7.2 160.3 %copy-start = (bf16[768,1536]{1,0:T(8,128)(2,1)S(1)}, bf16[768,1536]{1,0:T(8,128)(2,1)}, u32[]{:S(2)}) copy-start(bf16[768,1536]{1,0:T(8,128)(2,1)} %param.36) | copy-start | bytes 7077892
  7.2 5.5 copy-start.38
  7.2 5.5 copy-start.46
  7.2 155.7 %all-reduce.6.cloned.1.call-start = ((), (), s32[]{:S(2)}) async-start(), calls=%async_computation | async-start | bytes 9437184 | tf_op jit(solution)/shard_map/psum | solution.py:349
  7.3 5.4 copy-start.4
  7.3 8.0 %copy-start.24 = (bf16[768,384]{1,0:T(8,128)(2,1)S(1)}, bf16[768,384]{1,0:T(8,128)(2,1)}, u32[]{:S(2)}) copy-start(bf16[768,384]{1,0:T(8,128)(2,1)} %param.27) | copy-start | bytes 1769476
  7.3 8.0 %copy-start.62 = (f32[384]{0:T(512)S(1)}, f32[384]{0:T(512)}, u32[]{:S(2)}) copy-start(f32[384]{0:T(512)} %param.28) | copy-start | bytes 4612
  19.8 7.3 %copy-start.63 = (f32[384]{0:T(512)S(1)}, f32[384]{0:T(512)}, u32[]{:S(2)}) copy-start(f32[384]{0:T(512)} %param.31) | copy-start | bytes 4612
  31.7 9.1 %copy-start.23 = (pred[1536]{0:T(1024)(128)(4,1)}, pred[1536]{0:T(1024)(128)(4,1)S(1)}, u32[]{:S(2)}) copy-start(pred[1536]{0:T(1024)(128)(4,1)S(1)} %iota_compare_fusion.5) | copy-start | bytes 4612 | tf_op jit(solution)/shard_map/while
  62.5 9.1 %copy-start.23 = (pred[1536]{0:T(1024)(128)(4,1)}, pred[1536]{0:T(1024)(128)(4,1)S(1)}, u32[]{:S(2)}) copy-start(pred[1536]{0:T(1024)(128)(4,1)S(1)} %iota_compare_fusion.5) | copy-start | bytes 4612 | tf_op jit(solution)/shard_map/while
  93.2 9.1 %copy-start.23 = (pred[1536]{0:T(1024)(128)(4,1)}, pred[1536]{0:T(1024)(128)(4,1)S(1)}, u32[]{:S(2)}) copy-start(pred[1536]{0:T(1024)(128)(4,1)S(1)} %iota_compare_fusion.5) | copy-start | bytes 4612 | tf_op jit(solution)/shard_map/while
  130.9 32.0 %copy-start.55 = (f32[768]{0:T(1024)S(1)}, f32[768]{0:T(1024)}, u32[]{:S(2)}) copy-start(f32[768]{0:T(1024)} %param.33) | copy-start | bytes 9220
  130.9 88.7 %all-reduce.8.cloned.1.call-start = ((), (), s32[]{:S(2)}) async-start(), calls=%async_computation.1 | async-start | bytes 9437184 | tf_op jit(solution)/shard_map/psum | solution.py:368
  166.7 7.3 %copy-start.3 = (f32[1536,768]{1,0:T(8,128)}, f32[1536,768]{1,0:T(8,128)S(1)}, u32[]{:S(2)}) copy-start(f32[1536,768]{1,0:T(8,128)S(1)} %get-tuple-element.274) | copy-start | bytes 14155780
  166.8 58.7 %copy-start.34 = (f32[1536]{0:T(1024)}, f32[1536]{0:T(1024)S(1)}, u32[]{:S(2)}) copy-start(f32[1536]{0:T(1024)S(1)} %broadcast_multiply_fusion.4) | copy-start | bytes 18436
  167.5 58.0 %copy-start.36 = (f32[1536]{0:T(1024)}, f32[1536]{0:T(1024)S(1)}, u32[]{:S(2)}) copy-start(f32[1536]{0:T(1024)S(1)} %add_rsqrt_fusion) | copy-start | bytes 18436
  167.5 6.4 copy-start.13
  167.5 6.4 copy-start.49
  167.5 6.4 copy-start.57
  189.2 248.2 %all-reduce.10.cloned.1.call-start = ((), (), s32[]{:S(2)}) async-start(), calls=%async_computation.2 | async-start | bytes 18874368 | tf_op jit(solution)/shard_map/psum | solution.py:356
  219.6 5.8 copy-start.7
  219.6 5.9 copy-start.14
  219.6 5.9 copy-start.42
  219.7 5.9 copy-start.50
  225.5 7.2 %copy-start.16 = (bf16[384,768]{1,0:T(8,128)(2,1)S(1)}, bf16[384,768]{1,0:T(8,128)(2,1)}, u32[]{:S(2)}) copy-start(bf16[384,768]{1,0:T(8,128)(2,1)} %param.32) | copy-start | bytes 1769476
  244.4 11.9 %copy-start.64 = (bf16[1536,6,64]{0,2,1:T(8,128)(2,1)S(1)}, bf16[1536,6,64]{0,2,1:T(8,128)(2,1)}, u32[]{:S(2)}) copy-start(bf16[1536,6,64]{0,2,1:T(8,128)(2,1)} %get-tuple-element.470) | copy-start | bytes 3538948 | tf_op jit(solution)/shard_map/while
  267.5 6.5 copy-start.2
  289.3 11.9 %copy-start.64 = (bf16[1536,6,64]{0,2,1:T(8,128)(2,1)S(1)}, bf16[1536,6,64]{0,2,1:T(8,128)(2,1)}, u32[]{:S(2)}) copy-start(bf16[1536,6,64]{0,2,1:T(8,128)(2,1)} %get-tuple-element.470) | copy-start | bytes 3538948 | tf_op jit(solution)/shard_map/while
  312.3 6.5 copy-start.2
  334.8 11.9 %copy-start.64 = (bf16[1536,6,64]{0,2,1:T(8,128)(2,1)S(1)}, bf16[1536,6,64]{0,2,1:T(8,128)(2,1)}, u32[]{:S(2)}) copy-start(bf16[1536,6,64]{0,2,1:T(8,128)(2,1)} %get-tuple-element.470) | copy-start | bytes 3538948 | tf_op jit(solution)/shard_map/while
  357.8 6.5 copy-start.2
  380.7 4.7 copy-start.25
  387.1 4.7 copy-start.27
  397.0 14.3 %slice-start = ((s8[4718592]{0:T(1024)(128)(4,1)}), s8[4194304]{0:T(1024)(128)(4,1)S(1)}, s32[]{:S(2)}) async-start(s8[4718592]{0:T(1024)(128)(4,1)} %bitcast.221), calls=%async_computation.3 | async-start | bytes 8388608
  397.0 14.3 %slice-start.10 = ((s8[4718592]{0:T(1024)(128)(4,1)}), s8[4194304]{0:T(1024)(128)(4,1)S(1)}, s32[]{:S(2)}) async-start(s8[4718592]{0:T(1024)(128)(4,1)} %bitcast.245), calls=%async_computation.13 | async-start | bytes 8388608
  400.0 11.3 %slice-start.1 = ((s8[4718592]{0:T(1024)(128)(4,1)}), s8[524288]{0:T(1024)(128)(4,1)S(1)}, s32[]{:S(2)}) async-start(s8[4718592]{0:T(1024)(128)(4,1)} %bitcast.221), calls=%async_computation.4 | async-start | bytes 1048576
  400.0 11.3 %copy-start.35 = (f32[1536]{0:T(1024)S(1)}, f32[1536]{0:T(1024)}, u32[]{:S(2)}) copy-start(f32[1536]{0:T(1024)} %copy-done.34) | copy-start | bytes 18436
  400.0 11.3 %copy-start.37 = (f32[1536]{0:T(1024)S(1)}, f32[1536]{0:T(1024)}, u32[]{:S(2)}) copy-start(f32[1536]{0:T(1024)} %copy-done.36) | copy-start | bytes 18436
  400.0 11.3 %copy-start.43 = (f32[768]{0:T(1024)S(1)}, f32[768]{0:T(1024)}, u32[]{:S(2)}) copy-start(f32[768]{0:T(1024)} %param.34) | copy-start | bytes 9220
  400.0 11.3 %copy-start.61 = (f32[768]{0:T(1024)S(1)}, f32[768]{0:T(1024)}, u32[]{:S(2)}) copy-start(f32[768]{0:T(1024)} %param.35) | copy-start | bytes 9220
  400.1 11.3 %slice-start.11 = ((s8[4718592]{0:T(1024)(128)(4,1)}), s8[524288]{0:T(1024)(128)(4,1)S(1)}, s32[]{:S(2)}) async-start(s8[4718592]{0:T(1024)(128)(4,1)} %bitcast.245), calls=%async_computation.14 | async-start | bytes 1048576
  420.2 4.9 copy-start.12
  420.2 9.4 %copy-start.17 = (bf16[1536,768]{1,0:T(8,128)(2,1)S(1)}, bf16[1536,768]{1,0:T(8,128)(2,1)}, u32[]{:S(2)}) copy-start(bf16[1536,768]{1,0:T(8,128)(2,1)} %fusion.73) | copy-start | bytes 7077892
  420.2 11.8 %slice-start.4 = ((s8[4718592]{0:T(1024)(128)(4,1)}), s8[4194304]{0:T(1024)(128)(4,1)S(1)}, s32[]{:S(2)}) async-start(s8[4718592]{0:T(1024)(128)(4,1)} %bitcast.225), calls=%async_computation.7 | async-start | bytes 8388608
  425.1 7.0 %slice-start.5 = ((s8[4718592]{0:T(1024)(128)(4,1)}), s8[524288]{0:T(1024)(128)(4,1)S(1)}, s32[]{:S(2)}) async-start(s8[4718592]{0:T(1024)(128)(4,1)} %bitcast.225), calls=%async_computation.8 | async-start | bytes 1048576
  425.1 7.0 %copy-start.10 = (bf16[48,8,3,512]{3,1,2,0:T(8,128)(2,1)S(1)}, bf16[48,8,3,512]{3,1,2,0:T(8,128)(2,1)}, u32[]{:S(2)}) copy-start(bf16[48,8,3,512]{3,1,2,0:T(8,128)(2,1)} %copy-done.9) | copy-start | bytes 3538948
  432.1 5.4 copy-start.39
  434.2 7.2 %copy-start.40 = (f32[6912]{0:T(1024)S(1)}, f32[6912]{0:T(1024)}, u32[]{:S(2)}) copy-start(f32[6912]{0:T(1024)} %custom-call.2) | copy-start | bytes 82948
  434.2 7.2 %copy-start.52 = (f32[384]{0:T(512)S(1)}, f32[384]{0:T(512)}, u32[]{:S(2)}) copy-start(f32[384]{0:T(512)} %reduce_sum.187) | copy-start | bytes 4612
  434.2 7.3 %copy-start.53 = (f32[384]{0:T(512)S(1)}, f32[384]{0:T(512)}, u32[]{:S(2)}) copy-start(f32[384]{0:T(512)} %reduce_sum.189) | copy-start | bytes 4612
  434.2 7.3 %copy-start.48 = (f32[768]{0:T(1024)S(1)}, f32[768]{0:T(1024)}, u32[]{:S(2)}) copy-start(f32[768]{0:T(1024)} %get-tuple-element.271) | copy-start | bytes 9220
  434.2 7.3 %copy-start.45 = (f32[768]{0:T(1024)S(1)}, f32[768]{0:T(1024)}, u32[]{:S(2)}) copy-start(f32[768]{0:T(1024)} %get-tuple-element.225) | copy-start | bytes 9220
  434.2 7.3 %copy-start.44 = (f32[768]{0:T(1024)S(1)}, f32[768]{0:T(1024)}, u32[]{:S(2)}) copy-start(f32[768]{0:T(1024)} %get-tuple-element.231) | copy-start | bytes 9220
  434.2 7.3 %copy-start.54 = (f32[1536]{0:T(1024)S(1)}, f32[1536]{0:T(1024)}, u32[]{:S(2)}) copy-start(f32[1536]{0:T(1024)} %get-tuple-element.292) | copy-start | bytes 18436
  434.2 7.3 %copy-start.47 = (f32[768]{0:T(1024)S(1)}, f32[768]{0:T(1024)}, u32[]{:S(2)}) copy-start(f32[768]{0:T(1024)} %get-tuple-element.277) | copy-start | bytes 9220
  442.2 231.9 %slice-start.2 = ((s8[4718592]{0:T(1024)(128)(4,1)}), s8[524288]{0:T(1024)(128)(4,1)S(1)}, s32[]{:S(2)}) async-start(s8[4718592]{0:T(1024)(128)(4,1)} %bitcast.223), calls=%async_computation.5 | async-start | bytes 1048576
  664.1 10.0 %slice-start.3 = ((s8[4718592]{0:T(1024)(128)(4,1)}), s8[4194304]{0:T(1024)(128)(4,1)S(1)}, s32[]{:S(2)}) async-start(s8[4718592]{0:T(1024)(128)(4,1)} %bitcast.223), calls=%async_computation.6 | async-start | bytes 8388608
  668.3 5.8 copy-start.56
  668.3 14.5 %slice-start.8 = ((s8[4718592]{0:T(1024)(128)(4,1)}), s8[4194304]{0:T(1024)(128)(4,1)S(1)}, s32[]{:S(2)}) async-start(s8[4718592]{0:T(1024)(128)(4,1)} %bitcast.239), calls=%async_computation.11 | async-start | bytes 8388608
  674.1 4.6 copy-start.22
  674.1 5.6 copy-start.21
  674.1 8.6 %slice-start.9 = ((s8[4718592]{0:T(1024)(128)(4,1)}), s8[524288]{0:T(1024)(128)(4,1)S(1)}, s32[]{:S(2)}) async-start(s8[4718592]{0:T(1024)(128)(4,1)} %bitcast.239), calls=%async_computation.12 | async-start | bytes 1048576
  681.7 4.2 slice-start.6
  682.7 5.7 copy-start.1
  (27 other events, 56.1 us)
Sparse Core Ops, SparseCore 0:
  131.0 31.8 all-reduce.5
  189.3 30.3 all-reduce.7
  395.4 41.9 all-reduce.9

commit v2 on v0

v2 whole, which is shorter than its diff:
```python
import functools
import heapq
import math

import jax
import jax.numpy as jnp
from jax import lax
from jax.experimental import pallas as pl
from jax.experimental.pallas import tpu as pltpu
from jax.sharding import PartitionSpec as P

HD = 64
PAIR = 2 * HD
CHUNK = 512
BLOCK = 512
PIECE = 256

eps = 1e-05
score_scale = 0.125
masked_value = -1e30

MESH_ID = pl.DeviceIdType.MESH
NN = (((1,), (0,)), ((), ()))
NT = (((1,), (1,)), ((), ()))
TN = (((0,), (0,)), ((), ()))


def dot(left, right, form=NN):
    return lax.dot_general(left, right, form, preferred_element_type=jnp.float32)


def bit_of(index, bit):
    return (index // bit) % 2


def partner_of(index, bit):
    return index + bit - 2 * bit * bit_of(index, bit)


def dp_bits(size):
    return [1 << power for power in range(size.bit_length() - 1)]


def orders_of(size):
    bits = dp_bits(size)
    a, b, c, d = bits[:4]
    return [[a, b, c, d], [b, a, c, d], [c, a, b, d], [c, b, a, d]], bits[4:]


def landing_rows(rows, extra):
    return rows - (rows >> 4) + len(extra) * (rows >> 4)


class Unit:
    def __init__(self, buffer, total, place, shape, order, extra, landing, sems, me, core):
        (self.row, self.col), (self.total_row, self.total_col) = place
        self.rows, self.cols = shape
        self.buffer, self.total, self.landing = buffer, total, landing
        self.order, self.extra = order, extra
        self.send_sem, self.recv_sems, self.own_sem = sems
        self.me, self.core = me, core
        self.offsets = [0]
        self.lands = [0]
        for step, bit in enumerate(order):
            self.offsets.append(self.offsets[-1] + bit_of(me, bit) * (self.rows >> (step + 1)))
            self.lands.append(self.lands[-1] + (self.rows >> (step + 1)))
        self.stages = 2 * len(order) + len(extra)

    def held(self, offset, length):
        return (pl.ds(pl.multiple_of(self.row + offset, 8), length), pl.ds(self.col, self.cols))

    def final(self, offset, length):
        index = (pl.ds(pl.multiple_of(self.total_row + offset, 8), length), pl.ds(self.total_col, self.cols))
        return self.total.at[index]

    def landed(self, start, length):
        return (pl.ds(start, length), pl.ds(0, self.cols))

    def own_copy(self):
        length = self.rows >> len(self.order)
        return pltpu.make_async_copy(
            self.buffer.at[self.held(self.offsets[-1], length)],
            self.final(self.offsets[-1], length),
            self.own_sem,
        )

    def copy(self, stage):
        halvings = len(self.order)
        doublings = len(self.extra)
        if stage < halvings:
            bit = self.order[stage]
            length = self.rows >> (stage + 1)
            away = self.offsets[stage] + (1 - bit_of(self.me, bit)) * length
            source = self.buffer.at[self.held(away, length)]
            target = self.landing.at[self.landed(self.lands[stage], length)]
        elif stage < halvings + doublings:
            bit = self.extra[stage - halvings]
            length = self.rows >> halvings
            source = self.buffer.at[self.held(self.offsets[-1], length)]
            target = self.landing.at[self.landed(self.lands[-1] + (stage - halvings) * length, length)]
        else:
            step = 2 * halvings + doublings - 1 - stage
            bit = self.order[step]
            length = self.rows >> (step + 1)
            target = self.final(self.offsets[step + 1], length)
            source = target
            if step == halvings - 1:
                source = self.buffer.at[self.held(self.offsets[step + 1], length)]
        return pltpu.make_async_remote_copy(
            src_ref=source,
            dst_ref=target,
            send_sem=self.send_sem,
            recv_sem=self.recv_sems.at[stage],
            device_id=(partner_of(self.me, bit), self.core),
            device_id_type=MESH_ID,
        )

    def advance(self, stage):
        halvings = len(self.order)
        doublings = len(self.extra)
        if stage > 0:
            self.copy(stage - 1).wait()
            if stage <= halvings + doublings:
                step = min(stage, halvings)
                length = self.rows >> step
                if stage <= halvings:
                    land = self.lands[stage - 1]
                else:
                    land = self.lands[-1] + (stage - 1 - halvings) * length
                index = self.held(self.offsets[step], length)
                self.buffer[index] = self.buffer[index] + self.landing[self.landed(land, length)]
            if stage == halvings + doublings:
                self.own_copy().start()
            if stage == halvings + doublings + 1:
                self.own_copy().wait()
        if stage < self.stages:
            self.copy(stage).start()


def unit_table():
    table = []
    for j in range(3):
        for c in range(3):
            place = (CHUNK * j, 256 * c)
            table.append(("proj", place, place, (CHUNK, 256), c, ("hidden", j)))
        for c in range(3):
            place = (256 * c, CHUNK * j)
            table.append(("hidden", place, place, (256, CHUNK), c, ("hidden", j)))
    for c in range(3):
        table.append(("output", (0, 256 * c), (0, 256 * c), (384, 256), c, ("output", 0)))
    for name, col in (("query", 0), ("key", 384), ("value", 0)):
        for c in range(3):
            table.append((name, (256 * c, col), (256 * c, 0), (256, 384), c, ("attend", 0)))
    table.append(("small", (0, 0), (0, 0), (128, 128), 0, ("small", 0)))
    return table


def order_kind(number, kind):
    return kind if kind < 2 else 2 + (number // 3) % 2


def plan_units(size, ticks, table, freed):
    orders, extra = orders_of(size)
    bits = dp_bits(size)
    rate, delay, step_cost = 45e3, 2.5, 0.25
    free = {bit: 0.0 for bit in bits}

    def send(number, stage, now):
        _, _, _, (rows, cols), kind, _ = table[number]
        order = orders[order_kind(number, kind)]
        down = len(order)
        if stage < down:
            bit, length = order[stage], rows >> (stage + 1)
        elif stage < down + len(extra):
            bit, length = extra[stage - down], rows >> down
        else:
            step = 2 * down + len(extra) - 1 - stage
            bit, length = order[step], rows >> (step + 1)
        takes = length * cols * 4 / rate
        if bit == bits[3]:
            takes = 2 * takes
        free[bit] = max(free[bit], now) + takes
        if bit == bits[3]:
            free[bits[2]] = max(free[bits[2]], now) + takes / 2
        return free[bit] + delay

    stages = 8 + len(extra)
    waiting = []
    by_tick = {}
    for name, now in ticks:
        steps = []
        for number, entry in enumerate(table):
            if entry[5] == name:
                heapq.heappush(waiting, (now, number, 0))
        if name == ("free", 0):
            for item in sorted(waiting):
                ready, number, stage = item
                if number in freed and stage <= 5 + len(extra):
                    waiting.remove(item)
                    while stage <= 5 + len(extra):
                        now = max(now, ready) + step_cost
                        steps.append((number, stage))
                        ready = send(number, stage, now)
                        stage += 1
                    waiting.append((ready, number, stage))
            heapq.heapify(waiting)
        while waiting and waiting[0][0] <= now:
            _, number, stage = heapq.heappop(waiting)
            steps.append((number, stage))
            now += step_cost
            if stage < stages:
                heapq.heappush(waiting, (send(number, stage, now), number, stage + 1))
        by_tick[name] = steps
    left = []
    while waiting:
        ready, number, stage = heapq.heappop(waiting)
        now = max(now, ready) + step_cost
        left.append((number, stage))
        if stage < stages:
            heapq.heappush(waiting, (send(number, stage, now), number, stage + 1))
    return by_tick, left, now


def center_of(rows):
    center = rows - jnp.mean(rows, axis=-1, keepdims=True)
    inverse = lax.rsqrt(jnp.mean(center * center, axis=-1, keepdims=True) + eps)
    return center * inverse, inverse


def norm_back(grad_rows, unit_rows, inverse, norm_gain):
    scaled = grad_rows * norm_gain
    return inverse * (
        scaled
        - jnp.mean(scaled, axis=-1, keepdims=True)
        - unit_rows * jnp.mean(scaled * unit_rows, axis=-1, keepdims=True)
    )


def gelu_parts(before):
    normal_cdf = 0.5 * (1.0 + lax.erf(before * (1.0 / math.sqrt(2.0))))
    slope = normal_cdf + before * jnp.exp(-0.5 * before * before) * (1.0 / math.sqrt(2.0 * math.pi))
    return before * normal_cdf, slope


def column_sum(rows):
    return jnp.sum(rows, axis=0, keepdims=True)


def minus_in_three(column, first):
    lane = lax.broadcasted_iota(jnp.int32, (column.shape[0], PAIR), 1)
    high = (-column).astype(jnp.bfloat16).astype(jnp.float32)
    rest = -column - high
    middle = rest.astype(jnp.bfloat16).astype(jnp.float32)
    low = rest - middle
    zero = jnp.zeros((column.shape[0], PAIR), jnp.float32)
    tail = jnp.where(lane == 1, high, jnp.where(lane == 2, middle, jnp.where(lane == 3, low, zero)))
    return jnp.where(lane == 0, first, tail).astype(jnp.bfloat16)


SMALL = (("norm1_gain", 0, 768), ("norm1_bias", 1, 768), ("query_bias", 2, 384), ("value_bias", 3, 384),
         ("output_bias", 4, 768), ("norm2_gain", 5, 768), ("norm2_bias", 6, 768), ("hidden_bias", 7, 1536),
         ("proj_bias", 8, 768))
ROW_OF = {name: row for name, row, _ in SMALL}


def layer_kernel(size, length_ref, *refs):
    (
        frames_in, cotangent_in, hidden_weight_in, proj_weight_in,
        gain_one, shift_one, query_bias, value_bias, output_bias, gain_two, shift_two, hidden_bias, proj_bias,
        query_weight, key_weight, value_weight, output_weight,
    ) = refs[:17]
    (
        block_out, input_grad, query_sum, key_sum, value_sum, output_sum, proj_sum, hidden_sum, small_sum,
        peer_mlp, peer_two, peer_one,
    ) = refs[17:29]
    (
        left, right, resid, second, masked, hidden_w, proj_w, queries, keys, values, lse_terms, attended, key_terms,
        grad_proj, grad_hidden, land_proj, land_hidden, land_attend, land_output, land_small,
        fetched, staged, small, packed,
        load_sems, fetch_sem, stage_sem, peer_send, peer_recv, unit_send, unit_recv, unit_own,
    ) = refs[29:]
    me, core = lax.axis_index("dp"), lax.axis_index("tensor")
    total_rows = frames_in.shape[0]
    blocks, pieces = total_rows // BLOCK, total_rows // PIECE
    length = length_ref[0]
    orders, extra = orders_of(size)
    table = unit_table()

    loads = [
        pltpu.make_async_copy(source, target, load_sems.at[at])
        for at, (source, target) in enumerate(
            ((frames_in, second), (cotangent_in, masked), (hidden_weight_in, hidden_w), (proj_weight_in, proj_w))
        )
    ]
    for load in loads:
        load.start()
    barrier = pltpu.get_barrier_semaphore()
    for bit in dp_bits(size):
        pl.semaphore_signal(barrier, inc=1, device_id=(partner_of(me, bit), core), device_id_type=MESH_ID)
    pl.semaphore_signal(barrier, inc=1, device_id=(me, 1 - core), device_id_type=MESH_ID)

    held = {
        "proj": (grad_proj, proj_sum), "hidden": (grad_hidden, hidden_sum), "output": (resid, output_sum),
        "query": (grad_proj, query_sum), "key": (grad_proj, key_sum),
        "value": (grad_hidden, value_sum), "small": (packed, small_sum),
    }
    lands = {"proj": land_proj, "hidden": land_hidden, "output": land_output, "small": land_small}
    used = {}
    units = []
    for number, (name, place, total_place, shape, kind, _) in enumerate(table):
        shelf = lands.get(name, land_attend)
        key = name if name in lands else "attend"
        slot = used.get(key, 0)
        used[key] = slot + 1
        buffer, total = held[name]
        units.append(
            Unit(
                buffer, total, (place, total_place), shape, orders[order_kind(number, kind)], extra, shelf.at[slot],
                (unit_send.at[number], unit_recv.at[number], unit_own.at[number]), me, core,
            )
        )
    ticks, moment = [], 0.0
    for step in range(3 * blocks):
        moment += FFN_US
        ticks.append((("hidden", step // blocks) if step % blocks == blocks - 1 else ("ffn", step), moment))
    for step in range(pieces):
        moment += BACK_US
        ticks.append((("back", step), moment))
    moment += OUTPUT_US
    ticks.append((("output", 0), moment))
    for step in range(3 * pieces):
        moment += ATTEND_US
        ticks.append((("attn", step), moment))
    ticks.append((("free", 0), moment))
    for step in range(pieces):
        moment += FIRST_US
        ticks.append((("first", step) if step < pieces - 1 else ("attend", 0), moment))
    for step in range(pieces):
        moment += LAST_US
        ticks.append((("last", step) if step < pieces - 1 else ("small", 0), moment))
    freed = [
        at
        for at, (name, (row, col), _, _, _, _) in enumerate(table)
        if (name == "proj" and row < frames_in.shape[1]) or (name == "hidden" and col < 384)
    ]
    by_tick, remaining, _ = plan_units(size, ticks, table, freed)

    def run(steps):
        for number, stage in steps:
            units[number].advance(stage)

    def tick(step, count, name_of):
        for at in range(count):
            steps = by_tick[name_of(at)]
            if steps:
                @pl.when(step == at)
                def _(steps=steps):
                    run(steps)

    def to_peer(source, target, at):
        return pltpu.make_async_remote_copy(
            src_ref=source, dst_ref=target, send_sem=peer_send.at[at], recv_sem=peer_recv.at[at],
            device_id=(me, 1 - core), device_id_type=MESH_ID,
        )

    def rows_at(step, count):
        return pl.ds(pl.multiple_of(step * count, count), count)

    lane = lax.broadcasted_iota(jnp.int32, (1, PAIR), 1)
    heads = (lane < HD, lane >= HD)
    small[...] = jnp.zeros_like(small)
    packed[...] = jnp.zeros_like(packed)

    def add_small(name, value, at=0):
        row = ROW_OF[name]
        index = (slice(row, row + 1), pl.ds(at, value.shape[1]))
        small[index] = small[index] + value

    place = lax.broadcasted_iota(jnp.int32, (total_rows, PAIR), 0)
    column = lax.broadcasted_iota(jnp.int32, (total_rows, PAIR), 1)
    key_terms[...] = jnp.where(
        column == 0, jnp.where(place >= length, masked_value, 0.0), jnp.where(column < 4, 1.0, 0.0)
    ).astype(jnp.bfloat16)
    loads[0].wait()

    @pl.loop(0, blocks)
    def _(step):
        rows = rows_at(step, BLOCK)
        unit_rows, _ = center_of(second[rows, :].astype(jnp.float32))
        first_in = (unit_rows * gain_one[...] + shift_one[...]).astype(jnp.bfloat16)
        queries[rows, :] = ((dot(first_in, query_weight[...]) + query_bias[...]) * score_scale).astype(jnp.bfloat16)
        keys[rows, :] = dot(first_in, key_weight[...]).astype(jnp.bfloat16)
        values[rows, :] = (dot(first_in, value_weight[...]) + value_bias[...]).astype(jnp.bfloat16)

    first_term = jnp.where(lax.broadcasted_iota(jnp.int32, (BLOCK, PAIR), 1) == 0, 1.0, 0.0).astype(jnp.bfloat16)
    ones = jnp.ones((total_rows, PAIR), jnp.bfloat16)
    pl.semaphore_wait(barrier, len(dp_bits(size)) + 1)

    @pl.loop(0, blocks)
    def _(step):
        rows = rows_at(step, BLOCK)

        @pl.loop(0, 3)
        def _(pair):
            cols = pl.ds(pl.multiple_of(pair * PAIR, PAIR), PAIR)
            query_pair = queries[rows, cols]
            key_all = jnp.concatenate([keys[:, cols], key_terms[...]], axis=1)
            value_all = jnp.concatenate([values[:, cols], ones], axis=1)
            mixed = []
            for head in range(2):
                query_one = jnp.where(heads[head], query_pair, jnp.zeros_like(query_pair))
                scores = dot(jnp.concatenate([query_one, first_term], axis=1), key_all, NT)
                maxima = jnp.max(scores, axis=1, keepdims=True)
                weights = jnp.exp(scores - maxima).astype(jnp.bfloat16)
                mixture = dot(weights, value_all)
                totals = mixture[:, PAIR:]
                mixed.append(mixture[:, :PAIR] / totals)
                terms = minus_in_three(maxima + jnp.log(totals), 1.0)
                lse_terms[rows, pl.ds(pl.multiple_of((2 * pair + head) * PAIR, PAIR), PAIR)] = terms
            attended[rows, cols] = jnp.where(heads[0], mixed[0], mixed[1]).astype(jnp.bfloat16)

        right[rows, :] = dot(attended[rows, :], output_weight[...])
        to_peer(right.at[rows, :], left.at[rows, :], step).start()

    loads[1].wait()
    loads[2].wait()
    loads[3].wait()

    @pl.loop(0, 3 * blocks)
    def _(step):
        chunk, block = step // blocks, step % blocks
        rows = rows_at(block, BLOCK)
        units_of = rows_at(chunk, CHUNK)

        @pl.when(chunk == 0)
        def _():
            to_peer(right.at[rows, :], left.at[rows, :], block).wait()
            for half in range(BLOCK // PIECE):
                part = pl.ds(pl.multiple_of(block * BLOCK + half * PIECE, PIECE), PIECE)
                total = second[part, :].astype(jnp.float32) + (right[part, :] + left[part, :]) + output_bias[...]
                resid[part, :] = total
                unit_rows, _ = center_of(total)
                second[part, :] = (unit_rows * gain_two[...] + shift_two[...]).astype(jnp.bfloat16)
                live = lax.broadcasted_iota(jnp.int32, (PIECE, 1), 0) + (block * BLOCK + half * PIECE) < length
                grad_raw = masked[part, :]
                grad_f = jnp.where(live, grad_raw.astype(jnp.float32), 0.0)
                masked[part, :] = grad_f.astype(jnp.bfloat16)
                add_small("proj_bias", column_sum(grad_f))

        rows_in = second[rows, :]
        grad_in = masked[rows, :]
        up, down = hidden_w[:, units_of], proj_w[units_of, :]
        active_f, slope = gelu_parts(dot(rows_in, up) + hidden_bias[:, units_of])
        active = active_f.astype(jnp.bfloat16)
        grad_pre = dot(grad_in, down, NT) * slope
        grad_pre_b = grad_pre.astype(jnp.bfloat16)
        bias_at = (slice(ROW_OF["hidden_bias"], ROW_OF["hidden_bias"] + 1), units_of)
        small[bias_at] = small[bias_at] + column_sum(grad_pre)

        @pl.when(chunk == 0)
        def _():
            left[rows, :] = dot(active, down)
            right[rows, :] = dot(grad_pre_b, up, NT)

        @pl.when(chunk > 0)
        def _():
            left[rows, :] = left[rows, :] + dot(active, down)
            right[rows, :] = right[rows, :] + dot(grad_pre_b, up, NT)

        @pl.when(block == 0)
        def _():
            grad_proj[units_of, :] = dot(active, grad_in, TN)
            grad_hidden[:, units_of] = dot(rows_in, grad_pre_b, TN)

        @pl.when(block > 0)
        def _():
            grad_proj[units_of, :] = grad_proj[units_of, :] + dot(active, grad_in, TN)
            grad_hidden[:, units_of] = grad_hidden[:, units_of] + dot(rows_in, grad_pre_b, TN)

        @pl.when(chunk == 2)
        def _():
            for half in range(BLOCK // PIECE):
                piece = block * (BLOCK // PIECE) + half
                part = rows_at(piece, PIECE)
                to_peer(right.at[part, :], peer_two.at[part, :], blocks + piece).start()
                to_peer(left.at[part, :], peer_mlp.at[part, :], blocks + pieces + piece).start()

        tick(step, 3 * blocks, lambda at: ("hidden", at // blocks) if at % blocks == blocks - 1 else ("ffn", at))

    def fetch(source, part, at):
        return pltpu.make_async_copy(source.at[part, :], fetched.at[at], fetch_sem.at[at])

    def store(value, target, part):
        staged[...] = value.astype(jnp.bfloat16)
        copy = pltpu.make_async_copy(staged, target.at[part, :], stage_sem)
        copy.start()
        copy.wait()

    @pl.loop(0, pieces)
    def _(piece):
        part = rows_at(piece, PIECE)
        to_peer(right.at[part, :], peer_two.at[part, :], blocks + piece).wait()
        fetch(peer_two, part, 0).start()
        to_peer(left.at[part, :], peer_mlp.at[part, :], blocks + pieces + piece).wait()
        fetch(peer_mlp, part, 1).start()
        rows_f = resid[part, :]
        unit_rows, inverse = center_of(rows_f)
        fetch(peer_two, part, 0).wait()
        grad_two = right[part, :] + fetched[0]
        grad_rows = masked[part, :].astype(jnp.float32) + norm_back(grad_two, unit_rows, inverse, gain_two[...])
        add_small("norm2_gain", column_sum(grad_two * unit_rows))
        add_small("norm2_bias", column_sum(grad_two))
        add_small("output_bias", column_sum(grad_rows))
        right[part, :] = grad_rows
        grad_b = grad_rows.astype(jnp.bfloat16)
        masked[part, :] = grad_b
        proj_w[part, 0:384] = dot(grad_b, output_weight[...], NT).astype(jnp.bfloat16)
        fetch(peer_mlp, part, 1).wait()
        store(rows_f + (left[part, :] + fetched[1]) + proj_bias[...], block_out, part)
        tick(piece, pieces, lambda at: ("back", at))

    resid[0:384, :] = dot(attended[...], masked[...], TN)
    run(by_tick[("output", 0)])

    again = pltpu.make_async_copy(frames_in, masked, load_sems.at[4])
    again.start()
    for pair in range(3):
        hidden_w[pair * PAIR : (pair + 1) * PAIR, :] = keys[:, pair * PAIR : (pair + 1) * PAIR].T
    top = lax.broadcasted_iota(jnp.int32, (PAIR, 1), 0) < HD

    @pl.loop(0, 3 * pieces)
    def _(step):
        pair, piece = step // pieces, step % pieces
        part = rows_at(piece, PIECE)
        cols = pl.ds(pl.multiple_of(pair * PAIR, PAIR), PAIR)
        query_pair = queries[part, cols]
        grad_pair = proj_w[part, cols]
        product = grad_pair.astype(jnp.float32) * attended[part, cols].astype(jnp.float32)
        key_all = jnp.concatenate([keys[:, cols], key_terms[...]], axis=1)
        value_all = jnp.concatenate([values[:, cols], ones], axis=1)
        key_rows = hidden_w[cols, :]
        grad_values, grad_keys, grad_queries = 0.0, 0.0, []
        for head in range(2):
            mine = heads[head]
            query_one = jnp.where(mine, query_pair, jnp.zeros_like(query_pair))
            grad_one = jnp.where(mine, grad_pair, jnp.zeros_like(grad_pair))
            delta = jnp.sum(jnp.where(mine, product, 0.0), axis=1, keepdims=True)
            terms = lse_terms[part, pl.ds(pl.multiple_of((2 * pair + head) * PAIR, PAIR), PAIR)]
            probs = jnp.exp(dot(key_all, jnp.concatenate([query_one, terms], axis=1), NT))
            shifted = dot(value_all, jnp.concatenate([grad_one, minus_in_three(delta, 0.0)], axis=1), NT)
            grad_scores = (probs * shifted).astype(jnp.bfloat16)
            grad_values = grad_values + dot(probs.astype(jnp.bfloat16), grad_one)
            grad_keys = grad_keys + dot(grad_scores, query_one)
            grad_queries.append(dot(key_rows, grad_scores))
        grad_query = (jnp.where(top, grad_queries[0], grad_queries[1]) * score_scale).T
        second[part, cols] = grad_query.astype(jnp.bfloat16)
        bias_at = (slice(ROW_OF["query_bias"], ROW_OF["query_bias"] + 1), cols)
        small[bias_at] = small[bias_at] + column_sum(grad_query)

        @pl.when(piece == 0)
        def _():
            left[:, 0:PAIR] = grad_values
            left[:, PAIR : 2 * PAIR] = grad_keys

        @pl.when(piece > 0)
        def _():
            left[:, 0:PAIR] = left[:, 0:PAIR] + grad_values
            left[:, PAIR : 2 * PAIR] = left[:, PAIR : 2 * PAIR] + grad_keys

        @pl.when(piece == pieces - 1)
        def _():
            grad_all = left[:, 0:PAIR]
            bias_at = (slice(ROW_OF["value_bias"], ROW_OF["value_bias"] + 1), cols)
            small[bias_at] = column_sum(grad_all)
            proj_w[:, pl.ds(pl.multiple_of(384 + pair * PAIR, PAIR), PAIR)] = grad_all.astype(jnp.bfloat16)
            second[:, pl.ds(pl.multiple_of(384 + pair * PAIR, PAIR), PAIR)] = left[:, PAIR : 2 * PAIR].astype(
                jnp.bfloat16
            )

        tick(step, 3 * pieces, lambda at: ("attn", at))

    again.wait()
    run(by_tick[("free", 0)])

    @pl.loop(0, pieces)
    def _(piece):
        part = rows_at(piece, PIECE)
        unit_rows, _ = center_of(masked[part, :].astype(jnp.float32))
        first_in = (unit_rows * gain_one[...] + shift_one[...]).astype(jnp.bfloat16)
        grad_query, grad_key = second[part, 0:384], second[part, 384:768]
        grad_value = proj_w[part, 384:768]
        left[part, :] = (
            dot(grad_query, query_weight[...], NT)
            + dot(grad_key, key_weight[...], NT)
            + dot(grad_value, value_weight[...], NT)
        )
        to_peer(left.at[part, :], peer_one.at[part, :], blocks + 2 * pieces + piece).start()
        terms = [dot(first_in, grad, TN) for grad in (grad_query, grad_key, grad_value)]
        width = frames_in.shape[1]
        targets = (
            (grad_proj, (slice(0, width), slice(0, 384))),
            (grad_proj, (slice(0, width), slice(384, 768))),
            (grad_hidden, (slice(0, width), slice(0, 384))),
        )

        @pl.when(piece == 0)
        def _():
            for (ref, index), term in zip(targets, terms):
                ref[index] = term

        @pl.when(piece > 0)
        def _():
            for (ref, index), term in zip(targets, terms):
                ref[index] = ref[index] + term

        tick(piece, pieces, lambda at: ("first", at) if at < pieces - 1 else ("attend", 0))

    @pl.loop(0, pieces)
    def _(piece):
        part = rows_at(piece, PIECE)
        to_peer(left.at[part, :], peer_one.at[part, :], blocks + 2 * pieces + piece).wait()
        fetch(peer_one, part, 0).start()
        unit_rows, inverse = center_of(masked[part, :].astype(jnp.float32))
        fetch(peer_one, part, 0).wait()
        grad_one = left[part, :] + fetched[0]
        add_small("norm1_gain", column_sum(grad_one * unit_rows))
        add_small("norm1_bias", column_sum(grad_one))
        store(right[part, :] + norm_back(grad_one, unit_rows, inverse, gain_one[...]), input_grad, part)

        @pl.when(piece == pieces - 1)
        def _():
            at = 0
            for _, row, count in SMALL:
                for start in range(0, count, 128):
                    packed[at : at + 1, :] = small[row : row + 1, start : start + 128]
                    at += 1

        tick(piece, pieces, lambda at: ("last", at) if at < pieces - 1 else ("small", 0))

    run(remaining)


VMEM_BYTES = 64 * 2**20
FFN_US, BACK_US, OUTPUT_US, ATTEND_US, FIRST_US, LAST_US = 3.3, 2.0, 1.5, 2.8, 1.5, 1.5


def on_device(
    size,
    frames,
    lengths,
    cotangent,
    norm1_gain,
    norm1_bias,
    query_weight,
    query_bias,
    key_weight,
    value_weight,
    value_bias,
    output_weight,
    output_bias,
    norm2_gain,
    norm2_bias,
    hidden_weight,
    hidden_bias,
    proj_weight,
    proj_bias,
):
    rows, width = frames.shape[1:]
    part = query_weight.shape[1]
    hidden = hidden_weight.shape[1]
    extra = orders_of(size)[1]
    units = len(unit_table())
    stages = 8 + len(extra)
    pieces = rows // PIECE
    f32, bf16 = jnp.float32, jnp.bfloat16
    shape = jax.ShapeDtypeStruct
    anywhere = pl.BlockSpec(memory_space=pl.ANY)
    inside = pl.BlockSpec(memory_space=pltpu.VMEM)
    dma = pltpu.SemaphoreType.DMA
    results = pl.pallas_call(
        functools.partial(layer_kernel, size),
        out_shape=[
            shape((rows, width), bf16), shape((rows, width), bf16),
            shape((width, part), f32), shape((width, part), f32), shape((width, part), f32), shape((part, width), f32),
            shape((hidden, width), f32), shape((width, hidden), f32), shape((128, 128), f32),
            shape((rows, width), f32), shape((rows, width), f32), shape((rows, width), f32),
        ],
        in_specs=[pl.BlockSpec(memory_space=pltpu.SMEM)] + [anywhere] * 4 + [inside] * 13,
        out_specs=[anywhere] * 12,
        scratch_shapes=[
            pltpu.VMEM((rows, width), f32), pltpu.VMEM((rows, width), f32), pltpu.VMEM((rows, width), f32),
            pltpu.VMEM((rows, width), bf16), pltpu.VMEM((rows, width), bf16),
            pltpu.VMEM((width, hidden), bf16), pltpu.VMEM((hidden, width), bf16),
            pltpu.VMEM((rows, part), bf16), pltpu.VMEM((rows, part), bf16), pltpu.VMEM((rows, part), bf16),
            pltpu.VMEM((rows, 2 * part), bf16), pltpu.VMEM((rows, part), bf16), pltpu.VMEM((rows, PAIR), bf16),
            pltpu.VMEM((hidden, width), f32), pltpu.VMEM((width, hidden), f32),
            pltpu.VMEM((9, landing_rows(CHUNK, extra), 256), f32),
            pltpu.VMEM((9, landing_rows(256, extra), CHUNK), f32),
            pltpu.VMEM((9, landing_rows(256, extra), 384), f32),
            pltpu.VMEM((3, landing_rows(384, extra), 256), f32),
            pltpu.VMEM((1, landing_rows(128, extra), 128), f32),
            pltpu.VMEM((2, PIECE, width), f32), pltpu.VMEM((PIECE, width), bf16),
            pltpu.VMEM((16, hidden), f32), pltpu.VMEM((128, 128), f32),
            dma((5,)), dma((2,)), dma, dma((3 * pieces + rows // BLOCK,)), dma((3 * pieces + rows // BLOCK,)),
            dma((units,)), dma((units, stages)), dma((units,)),
        ],
        compiler_params=pltpu.CompilerParams(
            collective_id=0, has_side_effects=True, vmem_limit_bytes=VMEM_BYTES
        ),
        name="layer",
    )(
        lengths, frames[0], cotangent[0], hidden_weight, proj_weight,
        norm1_gain[None], norm1_bias[None], query_bias[None], value_bias[None], output_bias[None],
        norm2_gain[None], norm2_bias[None], hidden_bias[None], proj_bias[None],
        query_weight, key_weight, value_weight, output_weight,
    )
    block_out, input_grad, query_w, key_w, value_w, output_w, proj_w, hidden_w, packed = results[:9]
    flat = packed.reshape(-1)
    small, at = {}, 0
    for name, _, count in SMALL:
        small[name] = lax.slice(flat, (at,), (at + count,))
        at += count
    return (
        block_out[None], input_grad[None],
        small["norm1_gain"], small["norm1_bias"],
        query_w, small["query_bias"], key_w, value_w, small["value_bias"],
        output_w, small["output_bias"], small["norm2_gain"], small["norm2_bias"],
        hidden_w, small["hidden_bias"], proj_w, small["proj_bias"],
    )


def solution(mesh):
    placed = (
        P("dp", None, None),
        P("dp"),
        P("dp", None, None),
        P(),
        P(),
        P(None, "tensor"),
        P("tensor"),
        P(None, "tensor"),
        P(None, "tensor"),
        P("tensor"),
        P("tensor", None),
        P(),
        P(),
        P(),
        P(None, "tensor"),
        P("tensor"),
        P("tensor", None),
        P(),
    )
    return jax.shard_map(
        functools.partial(on_device, mesh.shape["dp"]),
        mesh=mesh,
        in_specs=placed,
        out_specs=(
            P("dp", None, None),
            P("dp", None, None),
            P(),
            P(),
            P(None, "tensor"),
            P("tensor"),
            P(None, "tensor"),
            P(None, "tensor"),
            P("tensor"),
            P("tensor", None),
            P(),
            P(),
            P(),
            P(None, "tensor"),
            P("tensor"),
            P("tensor", None),
            P(),
        ),
        check_vma=False,
    )
```

time: 878 us -> 299 us (0.34); the launches traced: 867 us -> 298 us
  waiting for transfers between devices: 373 us -> 0 us
  Pallas kernels: 0 us -> 266 us
  matrix products: 256 us -> 0 us
  other arithmetic: 87.6 us -> 0.01 us
  blocking collectives: 82.2 us -> 0 us
  local copies, waits for them, and re-layouts: 52 us -> 30.8 us
  between operations: 15.7 us -> 1.33 us
    psum x4 -> x0, waiting for transfers between devices: 373 us -> none  [the longest x1 312 us: on_device(): lax.psum((g_norm1_gain, g_norm1_bias, g_query_w, g_query_b, g_key_w, g_va...]
    pallas_call x0 -> x1, Pallas kernels: none -> 266 us  [on_device(): pl.pallas_call(functools.partial(layer_kernel, size), out_shape=[shape((r...]
    dot_general x39 -> x0, matrix products: 256 us -> none  [the longest x21 182 us: contract(): return jnp.einsum(form, left, right, preferred_element_type=jnp.float32)]
    psum x1 -> x0, blocking collectives: 82.2 us -> none  [on_device(): lax.psum((g_norm1_gain, g_norm1_bias, g_query_w, g_query_b, g_key_w, g_va...]
    reduce_sum x13 -> x0, other arithmetic: 64.6 us -> none  [the longest x3 30.6 us: per_block(): totals = jnp.sum(exponent, axis=-1, keepdims=True)]
    unnamed x150 -> x26, local copies, waits for them, and re-layouts: 31.7 us -> 15.3 us
    broadcast_in_dim x0 -> x9, local copies, waits for them, and re-layouts: none -> 11.4 us  [the longest x1 1.29 us: on_device(): hidden_bias[None]]
    broadcast_in_dim x5 -> x0, other arithmetic: 9.18 us -> none  [the longest x1 6.37 us: on_device(): block_out[None]]
  transfers between devices with their start and end apart: 4 -> 0, of which waited for: 4 -> 0; matrix products, arithmetic and copies ran while one was open for 6% -> 0% of each run, Pallas kernels for 0% -> 0%
where the time goes in v2:
time: 299 us; the launch traced here: 298 us
  Pallas kernels  266 us (89%)
  local copies, waits for them, and re-layouts  30.8 us (10%)
    pallas_call x1, Pallas kernels, on_device(): pl.pallas_call(functools.partial(layer_kernel, size), out_shape=[shape((r...  266 us
    unnamed x26, local copies, waits for them, and re-layouts  15.3 us

profile of v2, /device:TPU:0, one launch (start us, length us, event | category | flops | bytes accessed | tf_op | source)
XLA Modules:
  0.0 297.7 jit_solution(1052939718086550214)
XLA Ops:
  1.3 1.2 broadcast_in_dim.35.refs_6_
  2.5 1.2 broadcast_in_dim.36.refs_7_
  3.8 1.3 broadcast_in_dim.33.refs_4_
  5.1 1.3 broadcast_in_dim.34.refs_5_
  6.3 1.3 broadcast_in_dim.37.refs_8_
  7.6 1.3 broadcast_in_dim.38.refs_9_
  8.9 1.3 broadcast_in_dim.39.refs_10_
  10.1 1.3 broadcast_in_dim.41.refs_12_
  11.4 1.3 broadcast_in_dim.40.refs_11_
  12.7 265.6 %layer.1 = (bf16[1536,768]{1,0:T(8,128)(2,1)}, bf16[1536,768]{1,0:T(8,128)(2,1)}, f32[768,384]{1,0:T(8,128)}, f32[768,384]{1,0:T(8,128)}, f32[768,384]{1,0:T(8,1...) custom-call(s32[1]{0:T(128)S(6)} %copy.43.length_ref, ...), custom_call_target="tpu_custom_call" | custom-call | tf_op jit(solution)/shard_map/layer/pallas_call | solution.py:680
  278.3 1.3 slice_bitcast_fusion.7
  279.7 1.3 slice_bitcast_fusion
  281.0 0.0 copy-start
  281.0 1.5 slice_bitcast_fusion.1
  282.5 0.0 slice-start.2
  282.5 3.4 %copy.44 = bf16[1,1536,768]{2,1,0:T(8,128)(2,1)} copy(bf16[1,1536,768]{2,1,0:T(8,128)(2,1)} %bitcast.27) | data formatting | bytes 4718592
  285.8 0.0 copy-done
  285.8 0.0 copy-start.4
  285.8 0.0 copy-start.3
  285.8 1.4 copy.45
  287.2 0.7 copy-done.4
  287.9 0.0 copy-start.2
  287.9 0.0 slice-start.3
  287.9 1.0 copy.46
  289.0 0.0 copy-done.3
  289.0 0.0 copy-start.1
  289.0 1.0 copy.47
  290.0 0.0 copy-done.2
  290.0 1.0 copy.48
  291.0 0.0 copy-done.1
  291.0 0.0 slice-start
  291.0 1.0 copy.49
  292.0 0.0 slice-done.2
  292.0 0.0 slice-done.3
  292.0 0.0 slice-start.1
  292.0 2.4 copy.50
  294.4 0.8 slice-done
  295.2 0.3 slice-done.1
  295.6 2.2 copy.51
  (2 shorter events, 0.0 us)
Async XLA Ops:
  281.0 4.9 %copy-start = (bf16[1536,768]{1,0:T(8,128)(2,1)S(1)}, bf16[1536,768]{1,0:T(8,128)(2,1)}, u32[]{:S(2)}) copy-start(bf16[1536,768]{1,0:T(8,128)(2,1)} %get-tuple-element.27) | copy-start | bytes 7077892
  282.5 9.6 %slice-start.2 = ((s8[4718592]{0:T(1024)(128)(4,1)}), s8[4194304]{0:T(1024)(128)(4,1)S(1)}, s32[]{:S(2)}) async-start(s8[4718592]{0:T(1024)(128)(4,1)} %bitcast.24), calls=%async_computation.2 | async-start | bytes 8388608
  285.8 2.1 copy-start.4
  285.8 3.1 %copy-start.3 = (f32[768,384]{1,0:T(8,128)S(1)}, f32[768,384]{1,0:T(8,128)}, u32[]{:S(2)}) copy-start(f32[768,384]{1,0:T(8,128)} %get-tuple-element.66) | copy-start | bytes 3538948
  287.9 2.0 copy-start.2
  287.9 4.1 %slice-start.3 = ((s8[4718592]{0:T(1024)(128)(4,1)}), s8[524288]{0:T(1024)(128)(4,1)S(1)}, s32[]{:S(2)}) async-start(s8[4718592]{0:T(1024)(128)(4,1)} %bitcast.24), calls=%async_computation.3 | async-start | bytes 1048576
  289.0 2.0 copy-start.1
  291.0 4.2 %slice-start = ((s8[4718592]{0:T(1024)(128)(4,1)}), s8[4194304]{0:T(1024)(128)(4,1)S(1)}, s32[]{:S(2)}) async-start(s8[4718592]{0:T(1024)(128)(4,1)} %bitcast.22), calls=%async_computation | async-start | bytes 8388608
  292.0 3.5 %slice-start.1 = ((s8[4718592]{0:T(1024)(128)(4,1)}), s8[524288]{0:T(1024)(128)(4,1)S(1)}, s32[]{:S(2)}) async-start(s8[4718592]{0:T(1024)(128)(4,1)} %bitcast.22), calls=%async_computation.1 | async-start | bytes 1048576

commit v3 on v2

--- a/solution.py
+++ b/solution.py
@@ -1,5 +1,4 @@
 import functools
-import heapq
 import math
 
 import jax
@@ -11,7 +10,7 @@
 
 HD = 64
 PAIR = 2 * HD
-CHUNK = 512
+CHUNKS = ((256, 6),)
 BLOCK = 512
 PIECE = 256
 
@@ -137,15 +136,24 @@
             self.copy(stage).start()
 
 
+def chunk_list():
+    out, base = [], 0
+    for group, (width, count) in enumerate(CHUNKS):
+        for at in range(count):
+            out.append((group, at, base, width))
+            base += width
+    return out
+
+
 def unit_table():
     table = []
-    for j in range(3):
+    for number, (group, _, base, width) in enumerate(chunk_list()):
         for c in range(3):
-            place = (CHUNK * j, 256 * c)
-            table.append(("proj", place, place, (CHUNK, 256), c, ("hidden", j)))
+            place = (base, 256 * c)
+            table.append((("proj", group), place, place, (width, 256), c, ("hidden", number)))
         for c in range(3):
-            place = (256 * c, CHUNK * j)
-            table.append(("hidden", place, place, (256, CHUNK), c, ("hidden", j)))
+            place = (256 * c, base)
+            table.append((("hidden", group), place, place, (256, width), c, ("hidden", number)))
     for c in range(3):
         table.append(("output", (0, 256 * c), (0, 256 * c), (384, 256), c, ("output", 0)))
     for name, col in (("query", 0), ("key", 384), ("value", 0)):
@@ -159,65 +167,77 @@
     return kind if kind < 2 else 2 + (number // 3) % 2
 
 
-def plan_units(size, ticks, table, freed):
+def plan_units(size, ticks, table, freed, start):
     orders, extra = orders_of(size)
     bits = dp_bits(size)
-    rate, delay, step_cost = 45e3, 2.5, 0.25
-    free = {bit: 0.0 for bit in bits}
-
-    def send(number, stage, now):
+    rate, delay, step_cost, add_rate = RATES
+    spots = range(4)
+    busy = {}
+
+    def messages(number):
         _, _, _, (rows, cols), kind, _ = table[number]
         order = orders[order_kind(number, kind)]
-        down = len(order)
-        if stage < down:
-            bit, length = order[stage], rows >> (stage + 1)
-        elif stage < down + len(extra):
-            bit, length = extra[stage - down], rows >> down
-        else:
-            step = 2 * down + len(extra) - 1 - stage
-            bit, length = order[step], rows >> (step + 1)
-        takes = length * cols * 4 / rate
-        if bit == bits[3]:
-            takes = 2 * takes
-        free[bit] = max(free[bit], now) + takes
-        if bit == bits[3]:
-            free[bits[2]] = max(free[bits[2]], now) + takes / 2
-        return free[bit] + delay
-
-    stages = 8 + len(extra)
+        down = [(bit, (rows >> (step + 1)) * cols * 4) for step, bit in enumerate(order)]
+        across = [(bit, (rows >> len(order)) * cols * 4) for bit in extra]
+        return down + across + down[::-1], len(down) + len(across)
+
+    def arrival(message, now):
+        bit, length = message
+        takes, latest = length / rate, now
+        for spot in spots:
+            if bit == bits[2]:
+                path = [(min(spot, spot ^ 1), spot % 2)]
+            elif bit == bits[3]:
+                path = [(at, 0) for at in range(spot, spot + 2)] if spot < 2 else [
+                    (at, 1) for at in range(spot - 1, spot - 3, -1)
+                ]
+            else:
+                path = [(bit, spot)]
+            begin = now
+            for link in path:
+                key = (len(path) == 1 and bit != bits[2], link)
+                begin = max(busy.get(key, 0.0), begin)
+                busy[key] = begin + takes
+                latest = max(latest, begin + takes)
+        return latest + delay
+
+    plans = [messages(number) for number in range(len(table))]
     waiting = []
+
+    def take(item, now, steps):
+        waiting.remove(item)
+        _, number, stage = item
+        sent, downs = plans[number]
+        now += step_cost
+        if 0 < stage <= downs:
+            now += sent[stage - 1][1] / add_rate
+        steps.append((number, stage))
+        if stage < len(sent):
+            waiting.append((arrival(sent[stage], now), number, stage + 1))
+        return now
+
+    def run_ready(now, steps):
+        while True:
+            ready = [item for item in waiting if item[0] <= now]
+            if not ready:
+                return now
+            now = take(min(ready, key=urgency), now, steps)
+
     by_tick = {}
-    for name, now in ticks:
-        steps = []
-        for number, entry in enumerate(table):
-            if entry[5] == name:
-                heapq.heappush(waiting, (now, number, 0))
+    now = start
+    for name, takes in ticks:
+        steps = by_tick[name] = []
+        now += takes
+        waiting.extend((now, number, 0) for number, entry in enumerate(table) if entry[5] == name)
         if name == ("free", 0):
             for item in sorted(waiting):
-                ready, number, stage = item
-                if number in freed and stage <= 5 + len(extra):
-                    waiting.remove(item)
-                    while stage <= 5 + len(extra):
-                        now = max(now, ready) + step_cost
-                        steps.append((number, stage))
-                        ready = send(number, stage, now)
-                        stage += 1
-                    waiting.append((ready, number, stage))
-            heapq.heapify(waiting)
-        while waiting and waiting[0][0] <= now:
-            _, number, stage = heapq.heappop(waiting)
-            steps.append((number, stage))
-            now += step_cost
-            if stage < stages:
-                heapq.heappush(waiting, (send(number, stage, now), number, stage + 1))
-        by_tick[name] = steps
+                while item[1] in freed and item[2] <= 5 + len(extra):
+                    now = take(item, max(now, item[0]), steps)
+                    item = waiting[-1]
+        now = run_ready(now, steps)
     left = []
     while waiting:
-        ready, number, stage = heapq.heappop(waiting)
-        now = max(now, ready) + step_cost
-        left.append((number, stage))
-        if stage < stages:
-            heapq.heappush(waiting, (send(number, stage, now), number, stage + 1))
+        now = run_ready(max(now, min(waiting)[0]), left)
     return by_tick, left, now
 
 
@@ -257,26 +277,45 @@
     return jnp.where(lane == 0, first, tail).astype(jnp.bfloat16)
 
 
+class Row:
+    def __init__(self, ref):
+        self.ref = ref
+
+    def __getitem__(self, _):
+        return self.ref[...].reshape(1, self.ref.shape[0])
+
+
 SMALL = (("norm1_gain", 0, 768), ("norm1_bias", 1, 768), ("query_bias", 2, 384), ("value_bias", 3, 384),
          ("output_bias", 4, 768), ("norm2_gain", 5, 768), ("norm2_bias", 6, 768), ("hidden_bias", 7, 1536),
          ("proj_bias", 8, 768))
 ROW_OF = {name: row for name, row, _ in SMALL}
 
 
+def unpack_kernel(packed, *vectors):
+    at = 0
+    for (_, _, count), vector in zip(SMALL, vectors):
+        rows = count // 128
+        vector[...] = packed[at : at + rows, :].reshape(count)
+        at += rows
+
+
 def layer_kernel(size, length_ref, *refs):
     (
         frames_in, cotangent_in, hidden_weight_in, proj_weight_in,
         gain_one, shift_one, query_bias, value_bias, output_bias, gain_two, shift_two, hidden_bias, proj_bias,
-        query_weight, key_weight, value_weight, output_weight,
+        query_weight_in, key_weight_in, value_weight_in, output_weight_in,
     ) = refs[:17]
     (
         block_out, input_grad, query_sum, key_sum, value_sum, output_sum, proj_sum, hidden_sum, small_sum,
         peer_mlp, peer_two, peer_one,
     ) = refs[17:29]
+    gain_one, shift_one, query_bias, value_bias, output_bias, gain_two, shift_two, proj_bias = (
+        Row(ref) for ref in (gain_one, shift_one, query_bias, value_bias, output_bias, gain_two, shift_two, proj_bias)
+    )
     (
         left, right, resid, second, masked, hidden_w, proj_w, queries, keys, values, lse_terms, attended, key_terms,
-        grad_proj, grad_hidden, land_proj, land_hidden, land_attend, land_output, land_small,
-        fetched, staged, small, packed,
+        grad_proj, grad_hidden, *land_hidden, land_attend, land_output, land_small,
+        fetched, staged, small, packed, query_weight, key_weight, value_weight, output_weight,
         load_sems, fetch_sem, stage_sem, peer_send, peer_recv, unit_send, unit_recv, unit_own,
     ) = refs[29:]
     me, core = lax.axis_index("dp"), lax.axis_index("tensor")
@@ -284,15 +323,23 @@
     blocks, pieces = total_rows // BLOCK, total_rows // PIECE
     length = length_ref[0]
     orders, extra = orders_of(size)
+    chunks = chunk_list()
     table = unit_table()
 
+    pairs = [
+        (frames_in.at[pl.ds(block * BLOCK, BLOCK), :], second.at[pl.ds(block * BLOCK, BLOCK), :])
+        for block in range(blocks)
+    ]
+    pairs += [
+        (query_weight_in, query_weight), (key_weight_in, key_weight), (value_weight_in, value_weight),
+        (output_weight_in, output_weight), (cotangent_in, masked), (hidden_weight_in, hidden_w),
+        (proj_weight_in, proj_w), (frames_in, masked),
+    ]
     loads = [
-        pltpu.make_async_copy(source, target, load_sems.at[at])
-        for at, (source, target) in enumerate(
-            ((frames_in, second), (cotangent_in, masked), (hidden_weight_in, hidden_w), (proj_weight_in, proj_w))
-        )
+        pltpu.make_async_copy(source, target, load_sems.at[at]) for at, (source, target) in enumerate(pairs)
     ]
-    for load in loads:
+    first_loads, weight_loads, later_loads = loads[:blocks], loads[blocks : blocks + 3], loads[blocks + 3 : -1]
+    for load in first_loads + weight_loads:
         load.start()
     barrier = pltpu.get_barrier_semaphore()
     for bit in dp_bits(size):
@@ -300,11 +347,14 @@
     pl.semaphore_signal(barrier, inc=1, device_id=(me, 1 - core), device_id_type=MESH_ID)
 
     held = {
-        "proj": (grad_proj, proj_sum), "hidden": (grad_hidden, hidden_sum), "output": (resid, output_sum),
+        "output": (resid, output_sum),
         "query": (grad_proj, query_sum), "key": (grad_proj, key_sum),
         "value": (grad_hidden, value_sum), "small": (packed, small_sum),
     }
-    lands = {"proj": land_proj, "hidden": land_hidden, "output": land_output, "small": land_small}
+    lands = {"output": land_output, "small": land_small}
+    for group in range(len(CHUNKS)):
+        held["proj", group], held["hidden", group] = (grad_proj, proj_sum), (grad_hidden, hidden_sum)
+        lands["proj", group], lands["hidden", group] = land_hidden[2 * group : 2 * group + 2]
     used = {}
     units = []
     for number, (name, place, total_place, shape, kind, _) in enumerate(table):
@@ -319,31 +369,21 @@
                 (unit_send.at[number], unit_recv.at[number], unit_own.at[number]), me, core,
             )
         )
-    ticks, moment = [], 0.0
-    for step in range(3 * blocks):
-        moment += FFN_US
-        ticks.append((("hidden", step // blocks) if step % blocks == blocks - 1 else ("ffn", step), moment))
-    for step in range(pieces):
-        moment += BACK_US
-        ticks.append((("back", step), moment))
-    moment += OUTPUT_US
-    ticks.append((("output", 0), moment))
-    for step in range(3 * pieces):
-        moment += ATTEND_US
-        ticks.append((("attn", step), moment))
-    ticks.append((("free", 0), moment))
-    for step in range(pieces):
-        moment += FIRST_US
-        ticks.append((("first", step) if step < pieces - 1 else ("attend", 0), moment))
-    for step in range(pieces):
-        moment += LAST_US
-        ticks.append((("last", step) if step < pieces - 1 else ("small", 0), moment))
+    ticks = []
+    for number, (_, _, _, width) in enumerate(chunks):
+        for block in range(blocks):
+            name = ("hidden", number) if block == blocks - 1 else ("ffn", (number, block))
+            ticks.append((name, FFN_US * width / 512))
+    ticks += [(("back", step), BACK_US) for step in range(pieces)] + [(("output", 0), OUTPUT_US)]
+    ticks += [(("attn", step), ATTEND_US) for step in range(3 * pieces)] + [(("free", 0), 0.0)]
+    ticks += [(("first", step) if step < pieces - 1 else ("attend", 0), FIRST_US) for step in range(pieces)]
+    ticks += [(("last", step) if step < pieces - 1 else ("small", 0), LAST_US) for step in range(pieces)]
     freed = [
         at
         for at, (name, (row, col), _, _, _, _) in enumerate(table)
-        if (name == "proj" and row < frames_in.shape[1]) or (name == "hidden" and col < 384)
+        if (name[0] == "proj" and row < frames_in.shape[1]) or (name[0] == "hidden" and col < 384)
     ]
-    by_tick, remaining, _ = plan_units(size, ticks, table, freed)
+    by_tick, remaining, _ = plan_units(size, ticks, table, freed, 0.0)
 
     def run(steps):
         for number, stage in steps:
@@ -381,28 +421,31 @@
     key_terms[...] = jnp.where(
         column == 0, jnp.where(place >= length, masked_value, 0.0), jnp.where(column < 4, 1.0, 0.0)
     ).astype(jnp.bfloat16)
-    loads[0].wait()
+    for step in range(blocks):
+        first_loads[step].wait()
+        rows = pl.ds(step * BLOCK, BLOCK)
+        unit_rows, _ = center_of(second[rows, :].astype(jnp.float32))
+        first_in = (unit_rows * gain_one[...] + shift_one[...]).astype(jnp.bfloat16)
+        if step == 0:
+            for load in weight_loads:
+                load.wait()
+            for load in later_loads:
+                load.start()
+        queries[rows, :] = ((dot(first_in, query_weight[...]) + query_bias[...]) * score_scale).astype(jnp.bfloat16)
+        keys[rows, :] = dot(first_in, key_weight[...]).astype(jnp.bfloat16)
+        values[rows, :] = (dot(first_in, value_weight[...]) + value_bias[...]).astype(jnp.bfloat16)
+
+    first_term = jnp.where(lax.broadcasted_iota(jnp.int32, (BLOCK, PAIR), 1) == 0, 1.0, 0.0).astype(jnp.bfloat16)
+    ones = jnp.ones((total_rows, PAIR), jnp.bfloat16)
+    later_loads[0].wait()
+    pl.semaphore_wait(barrier, len(dp_bits(size)) + 1)
 
     @pl.loop(0, blocks)
     def _(step):
         rows = rows_at(step, BLOCK)
-        unit_rows, _ = center_of(second[rows, :].astype(jnp.float32))
-        first_in = (unit_rows * gain_one[...] + shift_one[...]).astype(jnp.bfloat16)
-        queries[rows, :] = ((dot(first_in, query_weight[...]) + query_bias[...]) * score_scale).astype(jnp.bfloat16)
-        keys[rows, :] = dot(first_in, key_weight[...]).astype(jnp.bfloat16)
-        values[rows, :] = (dot(first_in, value_weight[...]) + value_bias[...]).astype(jnp.bfloat16)
-
-    first_term = jnp.where(lax.broadcasted_iota(jnp.int32, (BLOCK, PAIR), 1) == 0, 1.0, 0.0).astype(jnp.bfloat16)
-    ones = jnp.ones((total_rows, PAIR), jnp.bfloat16)
-    pl.semaphore_wait(barrier, len(dp_bits(size)) + 1)
-
-    @pl.loop(0, blocks)
-    def _(step):
-        rows = rows_at(step, BLOCK)
-
-        @pl.loop(0, 3)
-        def _(pair):
-            cols = pl.ds(pl.multiple_of(pair * PAIR, PAIR), PAIR)
+
+        for pair in range(3):
+            cols = pl.ds(pair * PAIR, PAIR)
             query_pair = queries[rows, cols]
             key_all = jnp.concatenate([keys[:, cols], key_terms[...]], axis=1)
             value_all = jnp.concatenate([values[:, cols], ones], axis=1)
@@ -416,21 +459,22 @@
                 totals = mixture[:, PAIR:]
                 mixed.append(mixture[:, :PAIR] / totals)
                 terms = minus_in_three(maxima + jnp.log(totals), 1.0)
-                lse_terms[rows, pl.ds(pl.multiple_of((2 * pair + head) * PAIR, PAIR), PAIR)] = terms
+                lse_terms[rows, pl.ds((2 * pair + head) * PAIR, PAIR)] = terms
             attended[rows, cols] = jnp.where(heads[0], mixed[0], mixed[1]).astype(jnp.bfloat16)
 
         right[rows, :] = dot(attended[rows, :], output_weight[...])
         to_peer(right.at[rows, :], left.at[rows, :], step).start()
 
-    loads[1].wait()
-    loads[2].wait()
-    loads[3].wait()
-
-    @pl.loop(0, 3 * blocks)
-    def _(step):
-        chunk, block = step // blocks, step % blocks
+    for load in later_loads[1:]:
+        load.wait()
+
+    def feed_forward(group, step):
+        width, count = CHUNKS[group]
+        first = sum(chunk_count for _, chunk_count in CHUNKS[:group])
+        base = chunks[first][2]
+        chunk, block = first + step // blocks, step % blocks
         rows = rows_at(block, BLOCK)
-        units_of = rows_at(chunk, CHUNK)
+        units_of = pl.ds(pl.multiple_of(base + (step // blocks) * width, 256), width)
 
         @pl.when(chunk == 0)
         def _():
@@ -450,7 +494,7 @@
         rows_in = second[rows, :]
         grad_in = masked[rows, :]
         up, down = hidden_w[:, units_of], proj_w[units_of, :]
-        active_f, slope = gelu_parts(dot(rows_in, up) + hidden_bias[:, units_of])
+        active_f, slope = gelu_parts(dot(rows_in, up) + hidden_bias[units_of].reshape(1, width))
         active = active_f.astype(jnp.bfloat16)
         grad_pre = dot(grad_in, down, NT) * slope
         grad_pre_b = grad_pre.astype(jnp.bfloat16)
@@ -477,7 +521,7 @@
             grad_proj[units_of, :] = grad_proj[units_of, :] + dot(active, grad_in, TN)
             grad_hidden[:, units_of] = grad_hidden[:, units_of] + dot(rows_in, grad_pre_b, TN)
 
-        @pl.when(chunk == 2)
+        @pl.when(chunk == len(chunks) - 1)
         def _():
             for half in range(BLOCK // PIECE):
                 piece = block * (BLOCK // PIECE) + half
@@ -485,7 +529,14 @@
                 to_peer(right.at[part, :], peer_two.at[part, :], blocks + piece).start()
                 to_peer(left.at[part, :], peer_mlp.at[part, :], blocks + pieces + piece).start()
 
-        tick(step, 3 * blocks, lambda at: ("hidden", at // blocks) if at % blocks == blocks - 1 else ("ffn", at))
+        def name_of(at):
+            number = first + at // blocks
+            return ("hidden", number) if at % blocks == blocks - 1 else ("ffn", (number, at % blocks))
+
+        tick(step, count * blocks, name_of)
+
+    for group, (_, count) in enumerate(CHUNKS):
+        pl.loop(0, count * blocks)(functools.partial(feed_forward, group))
 
     def fetch(source, part, at):
         return pltpu.make_async_copy(source.at[part, :], fetched.at[at], fetch_sem.at[at])
@@ -522,7 +573,7 @@
     resid[0:384, :] = dot(attended[...], masked[...], TN)
     run(by_tick[("output", 0)])
 
-    again = pltpu.make_async_copy(frames_in, masked, load_sems.at[4])
+    again = loads[-1]
     again.start()
     for pair in range(3):
         hidden_w[pair * PAIR : (pair + 1) * PAIR, :] = keys[:, pair * PAIR : (pair + 1) * PAIR].T
@@ -641,7 +692,12 @@
 
 
 VMEM_BYTES = 64 * 2**20
-FFN_US, BACK_US, OUTPUT_US, ATTEND_US, FIRST_US, LAST_US = 3.3, 2.0, 1.5, 2.8, 1.5, 1.5
+FFN_US, BACK_US, OUTPUT_US, ATTEND_US, FIRST_US, LAST_US = 4.0, 1.4, 1.0, 2.5, 2.0, 2.0
+RATES = (46e3, 1.0, 0.05, 2e6)
+
+
+def urgency(item):
+    return (item[1], item[0])
 
 
 def on_device(
@@ -668,11 +724,15 @@
     rows, width = frames.shape[1:]
     part = query_weight.shape[1]
     hidden = hidden_weight.shape[1]
+    f32, bf16 = jnp.float32, jnp.bfloat16
     extra = orders_of(size)[1]
     units = len(unit_table())
+    chunk_lands = []
+    for chunk, count in CHUNKS:
+        chunk_lands.append(pltpu.VMEM((3 * count, landing_rows(chunk, extra), 256), f32))
+        chunk_lands.append(pltpu.VMEM((3 * count, landing_rows(256, extra), chunk), f32))
     stages = 8 + len(extra)
     pieces = rows // PIECE
-    f32, bf16 = jnp.float32, jnp.bfloat16
     shape = jax.ShapeDtypeStruct
     anywhere = pl.BlockSpec(memory_space=pl.ANY)
     inside = pl.BlockSpec(memory_space=pltpu.VMEM)
@@ -685,7 +745,7 @@
             shape((hidden, width), f32), shape((width, hidden), f32), shape((128, 128), f32),
             shape((rows, width), f32), shape((rows, width), f32), shape((rows, width), f32),
         ],
-        in_specs=[pl.BlockSpec(memory_space=pltpu.SMEM)] + [anywhere] * 4 + [inside] * 13,
+        in_specs=[pl.BlockSpec(memory_space=pltpu.SMEM)] + [anywhere] * 4 + [inside] * 9 + [anywhere] * 4,
         out_specs=[anywhere] * 12,
         scratch_shapes=[
             pltpu.VMEM((rows, width), f32), pltpu.VMEM((rows, width), f32), pltpu.VMEM((rows, width), f32),
@@ -694,14 +754,14 @@
             pltpu.VMEM((rows, part), bf16), pltpu.VMEM((rows, part), bf16), pltpu.VMEM((rows, part), bf16),
             pltpu.VMEM((rows, 2 * part), bf16), pltpu.VMEM((rows, part), bf16), pltpu.VMEM((rows, PAIR), bf16),
             pltpu.VMEM((hidden, width), f32), pltpu.VMEM((width, hidden), f32),
-            pltpu.VMEM((9, landing_rows(CHUNK, extra), 256), f32),
-            pltpu.VMEM((9, landing_rows(256, extra), CHUNK), f32),
+            *chunk_lands,
             pltpu.VMEM((9, landing_rows(256, extra), 384), f32),
             pltpu.VMEM((3, landing_rows(384, extra), 256), f32),
             pltpu.VMEM((1, landing_rows(128, extra), 128), f32),
             pltpu.VMEM((2, PIECE, width), f32), pltpu.VMEM((PIECE, width), bf16),
             pltpu.VMEM((16, hidden), f32), pltpu.VMEM((128, 128), f32),
-            dma((5,)), dma((2,)), dma, dma((3 * pieces + rows // BLOCK,)), dma((3 * pieces + rows // BLOCK,)),
+            *[pltpu.VMEM((width, part), bf16)] * 3, pltpu.VMEM((part, width), bf16),
+            dma((rows // BLOCK + 8,)), dma((2,)), dma, dma((3 * pieces + rows // BLOCK,)), dma((3 * pieces + rows // BLOCK,)),
             dma((units,)), dma((units, stages)), dma((units,)),
         ],
         compiler_params=pltpu.CompilerParams(
@@ -710,16 +770,15 @@
         name="layer",
     )(
         lengths, frames[0], cotangent[0], hidden_weight, proj_weight,
-        norm1_gain[None], norm1_bias[None], query_bias[None], value_bias[None], output_bias[None],
-        norm2_gain[None], norm2_bias[None], hidden_bias[None], proj_bias[None],
+        norm1_gain, norm1_bias, query_bias, value_bias, output_bias,
+        norm2_gain, norm2_bias, hidden_bias, proj_bias,
         query_weight, key_weight, value_weight, output_weight,
     )
     block_out, input_grad, query_w, key_w, value_w, output_w, proj_w, hidden_w, packed = results[:9]
-    flat = packed.reshape(-1)
-    small, at = {}, 0
-    for name, _, count in SMALL:
-        small[name] = lax.slice(flat, (at,), (at + count,))
-        at += count
+    vectors = pl.pallas_call(
+        unpack_kernel, out_shape=[shape((count,), f32) for _, _, count in SMALL], name="unpack"
+    )(packed)
+    small = {name: vector for (name, _, _), vector in zip(SMALL, vectors)}
     return (
         block_out[None], input_grad[None],
         small["norm1_gain"], small["norm1_bias"],

time: 299 us -> 271 us (0.906)
  local copies, waits for them, and re-layouts: 30.8 us -> 15.3 us
  Pallas kernels: 266 us -> 253 us
    pallas_call x1, Pallas kernels: 266 us -> 252 us  [on_device(): pl.pallas_call(functools.partial(layer_kernel, size), out_shape=[shape((r...]
    broadcast_in_dim x9 -> x0, local copies, waits for them, and re-layouts: 11.4 us -> none  [the longest x1 1.29 us: on_device(): hidden_bias[None]]
    slice x3 -> x0, local copies, waits for them, and re-layouts: 4.14 us -> none  [on_device(): small[name] = lax.slice(flat, (at,), (at + count,))]
where the time goes in v3:
time: 271 us; the launch traced here: 270 us
  Pallas kernels  253 us (93%)
  local copies, waits for them, and re-layouts  15.3 us (6%)
    pallas_call x1, Pallas kernels, on_device(): pl.pallas_call(functools.partial(layer_kernel, size), out_shape=[shape((r...  252 us
    unnamed x26, local copies, waits for them, and re-layouts  15.3 us

profile of v3, /device:TPU:0, one launch (start us, length us, event | category | flops | bytes accessed | tf_op | source)
XLA Modules:
  0.0 270.0 jit_solution(13816435612016414172)
XLA Ops:
  1.3 251.8 %layer.1 = (bf16[1536,768]{1,0:T(8,128)(2,1)}, bf16[1536,768]{1,0:T(8,128)(2,1)}, f32[768,384]{1,0:T(8,128)}, f32[768,384]{1,0:T(8,128)}, f32[768,384]{1,0:T(8,1...) custom-call(s32[1]{0:T(128)S(6)} %copy.43.length_ref, ...), custom_call_target="tpu_custom_call" | custom-call | tf_op jit(solution)/shard_map/layer/pallas_call | solution.py:740
  253.1 0.0 copy-start
  253.1 1.6 unpack.1
  254.7 0.0 slice-start.2
  254.7 3.4 %copy.44 = bf16[1,1536,768]{2,1,0:T(8,128)(2,1)} copy(bf16[1,1536,768]{2,1,0:T(8,128)(2,1)} %bitcast.9) | data formatting | bytes 4718592
  258.1 0.0 copy-done
  258.1 0.0 copy-start.4
  258.1 0.0 copy-start.3
  258.1 1.4 copy.45
  259.5 0.7 copy-done.4
  260.2 0.0 copy-start.2
  260.2 0.0 slice-start.3
  260.2 1.0 copy.46
  261.2 0.0 copy-done.3
  261.2 0.0 copy-start.1
  261.2 1.0 copy.47
  262.3 0.0 copy-done.2
  262.3 1.0 copy.48
  263.3 0.0 copy-done.1
  263.3 0.0 slice-start
  263.3 1.0 copy.49
  264.3 0.0 slice-done.2
  264.3 0.0 slice-done.3
  264.3 0.0 slice-start.1
  264.3 2.4 copy.50
  266.7 0.8 slice-done
  267.5 0.3 slice-done.1
  267.8 2.2 copy.51
  (2 shorter events, 0.0 us)
Async XLA Ops:
  253.1 5.0 %copy-start = (bf16[1536,768]{1,0:T(8,128)(2,1)S(1)}, bf16[1536,768]{1,0:T(8,128)(2,1)}, u32[]{:S(2)}) copy-start(bf16[1536,768]{1,0:T(8,128)(2,1)} %get-tuple-element.36) | copy-start | bytes 7077892
  254.7 9.5 %slice-start.2 = ((s8[4718592]{0:T(1024)(128)(4,1)}), s8[4194304]{0:T(1024)(128)(4,1)S(1)}, s32[]{:S(2)}) async-start(s8[4718592]{0:T(1024)(128)(4,1)} %bitcast.6), calls=%async_computation.2 | async-start | bytes 8388608
  258.1 2.1 copy-start.4
  258.1 3.1 %copy-start.3 = (f32[768,384]{1,0:T(8,128)S(1)}, f32[768,384]{1,0:T(8,128)}, u32[]{:S(2)}) copy-start(f32[768,384]{1,0:T(8,128)} %get-tuple-element.76) | copy-start | bytes 3538948
  260.2 2.0 copy-start.2
  260.2 4.1 %slice-start.3 = ((s8[4718592]{0:T(1024)(128)(4,1)}), s8[524288]{0:T(1024)(128)(4,1)S(1)}, s32[]{:S(2)}) async-start(s8[4718592]{0:T(1024)(128)(4,1)} %bitcast.6), calls=%async_computation.3 | async-start | bytes 1048576
  261.2 2.0 copy-start.1
  263.3 4.2 %slice-start = ((s8[4718592]{0:T(1024)(128)(4,1)}), s8[4194304]{0:T(1024)(128)(4,1)S(1)}, s32[]{:S(2)}) async-start(s8[4718592]{0:T(1024)(128)(4,1)} %bitcast.4), calls=%async_computation | async-start | bytes 8388608
  264.3 3.5 %slice-start.1 = ((s8[4718592]{0:T(1024)(128)(4,1)}), s8[524288]{0:T(1024)(128)(4,1)S(1)}, s32[]{:S(2)}) async-start(s8[4718592]{0:T(1024)(128)(4,1)} %bitcast.4), calls=%async_computation.1 | async-start | bytes 1048576

commit v4 on v3

--- a/solution.py
+++ b/solution.py
@@ -339,7 +339,7 @@
         pltpu.make_async_copy(source, target, load_sems.at[at]) for at, (source, target) in enumerate(pairs)
     ]
     first_loads, weight_loads, later_loads = loads[:blocks], loads[blocks : blocks + 3], loads[blocks + 3 : -1]
-    for load in first_loads + weight_loads:
+    for load in first_loads[:1] + weight_loads + first_loads[1:]:
         load.start()
     barrier = pltpu.get_barrier_semaphore()
     for bit in dp_bits(size):
@@ -421,16 +421,22 @@
     key_terms[...] = jnp.where(
         column == 0, jnp.where(place >= length, masked_value, 0.0), jnp.where(column < 4, 1.0, 0.0)
     ).astype(jnp.bfloat16)
+    def normed_block(step):
+        first_loads[step].wait()
+        unit_rows, _ = center_of(second[pl.ds(step * BLOCK, BLOCK), :].astype(jnp.float32))
+        return (unit_rows * gain_one[...] + shift_one[...]).astype(jnp.bfloat16)
+
+    upcoming = normed_block(0)
+    for load in weight_loads:
+        load.wait()
     for step in range(blocks):
-        first_loads[step].wait()
-        rows = pl.ds(step * BLOCK, BLOCK)
-        unit_rows, _ = center_of(second[rows, :].astype(jnp.float32))
-        first_in = (unit_rows * gain_one[...] + shift_one[...]).astype(jnp.bfloat16)
-        if step == 0:
-            for load in weight_loads:
-                load.wait()
+        first_in = upcoming
+        if step < blocks - 1:
+            upcoming = normed_block(step + 1)
+        if step == blocks - 2:
             for load in later_loads:
                 load.start()
+        rows = pl.ds(step * BLOCK, BLOCK)
         queries[rows, :] = ((dot(first_in, query_weight[...]) + query_bias[...]) * score_scale).astype(jnp.bfloat16)
         keys[rows, :] = dot(first_in, key_weight[...]).astype(jnp.bfloat16)
         values[rows, :] = (dot(first_in, value_weight[...]) + value_bias[...]).astype(jnp.bfloat16)
@@ -444,23 +450,28 @@
     def _(step):
         rows = rows_at(step, BLOCK)
 
-        for pair in range(3):
-            cols = pl.ds(pair * PAIR, PAIR)
+        def scores_of(number):
+            cols = pl.ds((number // 2) * PAIR, PAIR)
             query_pair = queries[rows, cols]
+            query_one = jnp.where(heads[number % 2], query_pair, jnp.zeros_like(query_pair))
             key_all = jnp.concatenate([keys[:, cols], key_terms[...]], axis=1)
-            value_all = jnp.concatenate([values[:, cols], ones], axis=1)
-            mixed = []
-            for head in range(2):
-                query_one = jnp.where(heads[head], query_pair, jnp.zeros_like(query_pair))
-                scores = dot(jnp.concatenate([query_one, first_term], axis=1), key_all, NT)
-                maxima = jnp.max(scores, axis=1, keepdims=True)
-                weights = jnp.exp(scores - maxima).astype(jnp.bfloat16)
-                mixture = dot(weights, value_all)
-                totals = mixture[:, PAIR:]
-                mixed.append(mixture[:, :PAIR] / totals)
-                terms = minus_in_three(maxima + jnp.log(totals), 1.0)
-                lse_terms[rows, pl.ds((2 * pair + head) * PAIR, PAIR)] = terms
-            attended[rows, cols] = jnp.where(heads[0], mixed[0], mixed[1]).astype(jnp.bfloat16)
+            return dot(jnp.concatenate([query_one, first_term], axis=1), key_all, NT)
+
+        mixed = []
+        upcoming = scores_of(0)
+        for number in range(6):
+            scores = scores_of(number) if extra and number else upcoming
+            if number < 5 and not extra:
+                upcoming = scores_of(number + 1)
+            cols = pl.ds((number // 2) * PAIR, PAIR)
+            maxima = jnp.max(scores, axis=1, keepdims=True)
+            weights = jnp.exp(scores - maxima).astype(jnp.bfloat16)
+            mixture = dot(weights, jnp.concatenate([values[:, cols], ones], axis=1))
+            totals = mixture[:, PAIR:]
+            mixed.append(mixture[:, :PAIR] / totals)
+            lse_terms[rows, pl.ds(number * PAIR, PAIR)] = minus_in_three(maxima + jnp.log(totals), 1.0)
+            if number % 2:
+                attended[rows, cols] = jnp.where(heads[0], mixed[-2], mixed[-1]).astype(jnp.bfloat16)
 
         right[rows, :] = dot(attended[rows, :], output_weight[...])
         to_peer(right.at[rows, :], left.at[rows, :], step).start()

time: 271 us -> 268 us (0.989)
  no operation moved by 1% of the time
where the time goes in v4:
time: 268 us; the launch traced here: 267 us
  Pallas kernels  251 us (94%)
  local copies, waits for them, and re-layouts  15.3 us (6%)
    pallas_call x1, Pallas kernels, on_device(): pl.pallas_call(functools.partial(layer_kernel, size), out_shape=[shape((r...  249 us
    unnamed x26, local copies, waits for them, and re-layouts  15.3 us

profile of v4, /device:TPU:0, one launch (start us, length us, event | category | flops | bytes accessed | tf_op | source)
XLA Modules:
  0.0 267.5 jit_solution(12951078920337910569)
XLA Ops:
  1.3 249.3 %layer.1 = (bf16[1536,768]{1,0:T(8,128)(2,1)}, bf16[1536,768]{1,0:T(8,128)(2,1)}, f32[768,384]{1,0:T(8,128)}, f32[768,384]{1,0:T(8,128)}, f32[768,384]{1,0:T(8,1...) custom-call(s32[1]{0:T(128)S(6)} %copy.43.length_ref, ...), custom_call_target="tpu_custom_call" | custom-call | tf_op jit(solution)/shard_map/layer/pallas_call | solution.py:751
  250.6 0.0 copy-start
  250.6 1.6 unpack.1
  252.2 0.0 slice-start.2
  252.2 3.4 %copy.44 = bf16[1,1536,768]{2,1,0:T(8,128)(2,1)} copy(bf16[1,1536,768]{2,1,0:T(8,128)(2,1)} %bitcast.9) | data formatting | bytes 4718592
  255.6 0.0 copy-done
  255.6 0.0 copy-start.4
  255.6 0.0 copy-start.3
  255.6 1.4 copy.45
  257.0 0.7 copy-done.4
  257.7 0.0 copy-start.2
  257.7 0.0 slice-start.3
  257.7 1.0 copy.46
  258.7 0.0 copy-done.3
  258.7 0.0 copy-start.1
  258.7 1.0 copy.47
  259.7 0.0 copy-done.2
  259.7 1.0 copy.48
  260.7 0.0 copy-done.1
  260.7 0.0 slice-start
  260.7 1.0 copy.49
  261.8 0.0 slice-done.2
  261.8 0.0 slice-done.3
  261.8 0.0 slice-start.1
  261.8 2.4 copy.50
  264.2 0.8 slice-done
  265.0 0.3 slice-done.1
  265.3 2.2 copy.51
  (2 shorter events, 0.0 us)
Async XLA Ops:
  250.6 5.0 %copy-start = (bf16[1536,768]{1,0:T(8,128)(2,1)S(1)}, bf16[1536,768]{1,0:T(8,128)(2,1)}, u32[]{:S(2)}) copy-start(bf16[1536,768]{1,0:T(8,128)(2,1)} %get-tuple-element.36) | copy-start | bytes 7077892
  252.2 9.5 %slice-start.2 = ((s8[4718592]{0:T(1024)(128)(4,1)}), s8[4194304]{0:T(1024)(128)(4,1)S(1)}, s32[]{:S(2)}) async-start(s8[4718592]{0:T(1024)(128)(4,1)} %bitcast.6), calls=%async_computation.2 | async-start | bytes 8388608
  255.6 2.1 copy-start.4
  255.6 3.1 %copy-start.3 = (f32[768,384]{1,0:T(8,128)S(1)}, f32[768,384]{1,0:T(8,128)}, u32[]{:S(2)}) copy-start(f32[768,384]{1,0:T(8,128)} %get-tuple-element.76) | copy-start | bytes 3538948
  257.7 2.0 copy-start.2
  257.7 4.1 %slice-start.3 = ((s8[4718592]{0:T(1024)(128)(4,1)}), s8[524288]{0:T(1024)(128)(4,1)S(1)}, s32[]{:S(2)}) async-start(s8[4718592]{0:T(1024)(128)(4,1)} %bitcast.6), calls=%async_computation.3 | async-start | bytes 1048576
  258.7 2.0 copy-start.1
  260.7 4.2 %slice-start = ((s8[4718592]{0:T(1024)(128)(4,1)}), s8[4194304]{0:T(1024)(128)(4,1)S(1)}, s32[]{:S(2)}) async-start(s8[4718592]{0:T(1024)(128)(4,1)} %bitcast.4), calls=%async_computation | async-start | bytes 8388608
  261.8 3.5 %slice-start.1 = ((s8[4718592]{0:T(1024)(128)(4,1)}), s8[524288]{0:T(1024)(128)(4,1)S(1)}, s32[]{:S(2)}) async-start(s8[4718592]{0:T(1024)(128)(4,1)} %bitcast.4), calls=%async_computation.1 | async-start | bytes 1048576

commit v5 on v4

--- a/solution.py
+++ b/solution.py
@@ -10,7 +10,7 @@
 
 HD = 64
 PAIR = 2 * HD
-CHUNKS = ((256, 6),)
+CHUNKS = ((256, 2), (512, 2))
 BLOCK = 512
 PIECE = 256
 
@@ -43,7 +43,11 @@
 def orders_of(size):
     bits = dp_bits(size)
     a, b, c, d = bits[:4]
-    return [[a, b, c, d], [b, a, c, d], [c, a, b, d], [c, b, a, d]], bits[4:]
+    orders = [
+        [a, b, c, d], [b, a, c, d], [c, a, b, d], [c, b, a, d],
+        [a, c, b, d], [b, c, a, d], [c, d, a, b], [c, d, b, a],
+    ]
+    return orders, bits[4:]
 
 
 def landing_rows(rows, extra):
@@ -150,21 +154,17 @@
     for number, (group, _, base, width) in enumerate(chunk_list()):
         for c in range(3):
             place = (base, 256 * c)
-            table.append((("proj", group), place, place, (width, 256), c, ("hidden", number)))
+            table.append((("proj", group), place, place, (width, 256), ("hidden", number)))
         for c in range(3):
             place = (256 * c, base)
-            table.append((("hidden", group), place, place, (256, width), c, ("hidden", number)))
+            table.append((("hidden", group), place, place, (256, width), ("hidden", number)))
     for c in range(3):
-        table.append(("output", (0, 256 * c), (0, 256 * c), (384, 256), c, ("output", 0)))
+        table.append(("output", (0, 256 * c), (0, 256 * c), (384, 256), ("output", 0)))
     for name, col in (("query", 0), ("key", 384), ("value", 0)):
         for c in range(3):
-            table.append((name, (256 * c, col), (256 * c, 0), (256, 384), c, ("attend", 0)))
-    table.append(("small", (0, 0), (0, 0), (128, 128), 0, ("small", 0)))
+            table.append((name, (256 * c, col), (256 * c, 0), (256, 384), ("attend", 0)))
+    table.append(("small", (0, 0), (0, 0), (128, 128), ("small", 0)))
     return table
-
-
-def order_kind(number, kind):
-    return kind if kind < 2 else 2 + (number // 3) % 2
 
 
 def plan_units(size, ticks, table, freed, start):
@@ -175,8 +175,8 @@
     busy = {}
 
     def messages(number):
-        _, _, _, (rows, cols), kind, _ = table[number]
-        order = orders[order_kind(number, kind)]
+        _, _, _, (rows, cols), _ = table[number]
+        order = orders[KINDS[number]]
         down = [(bit, (rows >> (step + 1)) * cols * 4) for step, bit in enumerate(order)]
         across = [(bit, (rows >> len(order)) * cols * 4) for bit in extra]
         return down + across + down[::-1], len(down) + len(across)
@@ -228,7 +228,7 @@
     for name, takes in ticks:
         steps = by_tick[name] = []
         now += takes
-        waiting.extend((now, number, 0) for number, entry in enumerate(table) if entry[5] == name)
+        waiting.extend((now, number, 0) for number, entry in enumerate(table) if entry[4] == name)
         if name == ("free", 0):
             for item in sorted(waiting):
                 while item[1] in freed and item[2] <= 5 + len(extra):
@@ -302,9 +302,11 @@
 def layer_kernel(size, length_ref, *refs):
     (
         frames_in, cotangent_in, hidden_weight_in, proj_weight_in,
-        gain_one, shift_one, query_bias, value_bias, output_bias, gain_two, shift_two, hidden_bias, proj_bias,
+        *vectors_in,
         query_weight_in, key_weight_in, value_weight_in, output_weight_in,
     ) = refs[:17]
+    vectors = refs[-9:]
+    gain_one, shift_one, query_bias, value_bias, output_bias, gain_two, shift_two, hidden_bias, proj_bias = vectors
     (
         block_out, input_grad, query_sum, key_sum, value_sum, output_sum, proj_sum, hidden_sum, small_sum,
         peer_mlp, peer_two, peer_one,
@@ -317,7 +319,7 @@
         grad_proj, grad_hidden, *land_hidden, land_attend, land_output, land_small,
         fetched, staged, small, packed, query_weight, key_weight, value_weight, output_weight,
         load_sems, fetch_sem, stage_sem, peer_send, peer_recv, unit_send, unit_recv, unit_own,
-    ) = refs[29:]
+    ) = refs[29:-9]
     me, core = lax.axis_index("dp"), lax.axis_index("tensor")
     total_rows = frames_in.shape[0]
     blocks, pieces = total_rows // BLOCK, total_rows // PIECE
@@ -339,7 +341,12 @@
         pltpu.make_async_copy(source, target, load_sems.at[at]) for at, (source, target) in enumerate(pairs)
     ]
     first_loads, weight_loads, later_loads = loads[:blocks], loads[blocks : blocks + 3], loads[blocks + 3 : -1]
-    for load in first_loads[:1] + weight_loads + first_loads[1:]:
+    vector_loads = [
+        pltpu.make_async_copy(source, target, load_sems.at[len(pairs) + at])
+        for at, (source, target) in enumerate(zip(vectors_in, vectors))
+    ]
+    weight_loads = vector_loads + weight_loads
+    for load in vector_loads + first_loads[:1] + weight_loads[9:] + first_loads[1:]:
         load.start()
     barrier = pltpu.get_barrier_semaphore()
     for bit in dp_bits(size):
@@ -357,7 +364,7 @@
         lands["proj", group], lands["hidden", group] = land_hidden[2 * group : 2 * group + 2]
     used = {}
     units = []
-    for number, (name, place, total_place, shape, kind, _) in enumerate(table):
+    for number, (name, place, total_place, shape, _) in enumerate(table):
         shelf = lands.get(name, land_attend)
         key = name if name in lands else "attend"
         slot = used.get(key, 0)
@@ -365,7 +372,7 @@
         buffer, total = held[name]
         units.append(
             Unit(
-                buffer, total, (place, total_place), shape, orders[order_kind(number, kind)], extra, shelf.at[slot],
+                buffer, total, (place, total_place), shape, orders[KINDS[number]], extra, shelf.at[slot],
                 (unit_send.at[number], unit_recv.at[number], unit_own.at[number]), me, core,
             )
         )
@@ -373,14 +380,14 @@
     for number, (_, _, _, width) in enumerate(chunks):
         for block in range(blocks):
             name = ("hidden", number) if block == blocks - 1 else ("ffn", (number, block))
-            ticks.append((name, FFN_US * width / 512))
+            ticks.append((name, FFN_US if width == 256 else 1.57 * FFN_US))
     ticks += [(("back", step), BACK_US) for step in range(pieces)] + [(("output", 0), OUTPUT_US)]
     ticks += [(("attn", step), ATTEND_US) for step in range(3 * pieces)] + [(("free", 0), 0.0)]
     ticks += [(("first", step) if step < pieces - 1 else ("attend", 0), FIRST_US) for step in range(pieces)]
     ticks += [(("last", step) if step < pieces - 1 else ("small", 0), LAST_US) for step in range(pieces)]
     freed = [
         at
-        for at, (name, (row, col), _, _, _, _) in enumerate(table)
+        for at, (name, (row, col), _, _, _) in enumerate(table)
         if (name[0] == "proj" and row < frames_in.shape[1]) or (name[0] == "hidden" and col < 384)
     ]
     by_tick, remaining, _ = plan_units(size, ticks, table, freed, 0.0)
@@ -410,6 +417,8 @@
     heads = (lane < HD, lane >= HD)
     small[...] = jnp.zeros_like(small)
     packed[...] = jnp.zeros_like(packed)
+    grad_proj[...] = jnp.zeros_like(grad_proj)
+    grad_hidden[...] = jnp.zeros_like(grad_hidden)
 
     def add_small(name, value, at=0):
         row = ROW_OF[name]
@@ -426,8 +435,10 @@
         unit_rows, _ = center_of(second[pl.ds(step * BLOCK, BLOCK), :].astype(jnp.float32))
         return (unit_rows * gain_one[...] + shift_one[...]).astype(jnp.bfloat16)
 
+    for load in vector_loads:
+        load.wait()
     upcoming = normed_block(0)
-    for load in weight_loads:
+    for load in weight_loads[9:]:
         load.wait()
     for step in range(blocks):
         first_in = upcoming
@@ -494,6 +505,8 @@
                 part = pl.ds(pl.multiple_of(block * BLOCK + half * PIECE, PIECE), PIECE)
                 total = second[part, :].astype(jnp.float32) + (right[part, :] + left[part, :]) + output_bias[...]
                 resid[part, :] = total
+                left[part, :] = jnp.zeros((PIECE, left.shape[1]), jnp.float32)
+                right[part, :] = jnp.zeros((PIECE, left.shape[1]), jnp.float32)
                 unit_rows, _ = center_of(total)
                 second[part, :] = (unit_rows * gain_two[...] + shift_two[...]).astype(jnp.bfloat16)
                 live = lax.broadcasted_iota(jnp.int32, (PIECE, 1), 0) + (block * BLOCK + half * PIECE) < length
@@ -502,35 +515,26 @@
                 masked[part, :] = grad_f.astype(jnp.bfloat16)
                 add_small("proj_bias", column_sum(grad_f))
 
-        rows_in = second[rows, :]
-        grad_in = masked[rows, :]
         up, down = hidden_w[:, units_of], proj_w[units_of, :]
-        active_f, slope = gelu_parts(dot(rows_in, up) + hidden_bias[units_of].reshape(1, width))
-        active = active_f.astype(jnp.bfloat16)
-        grad_pre = dot(grad_in, down, NT) * slope
-        grad_pre_b = grad_pre.astype(jnp.bfloat16)
+        bias = hidden_bias[units_of].reshape(1, width)
+        halves = [
+            pl.ds(pl.multiple_of(block * BLOCK + half * PIECE, PIECE), PIECE) for half in range(BLOCK // PIECE)
+        ]
+        products = [(dot(second[part, :], up) + bias, dot(masked[part, :], down, NT)) for part in halves]
+        actives, grads, bias_grad = [], [], 0.0
+        for part, (before, grad_active) in zip(halves, products):
+            active_f, slope = gelu_parts(before)
+            grad_pre = grad_active * slope
+            actives.append(active_f.astype(jnp.bfloat16))
+            grads.append(grad_pre.astype(jnp.bfloat16))
+            bias_grad = bias_grad + column_sum(grad_pre)
+            left[part, :] = left[part, :] + dot(actives[-1], down)
+            right[part, :] = right[part, :] + dot(grads[-1], up, NT)
         bias_at = (slice(ROW_OF["hidden_bias"], ROW_OF["hidden_bias"] + 1), units_of)
-        small[bias_at] = small[bias_at] + column_sum(grad_pre)
-
-        @pl.when(chunk == 0)
-        def _():
-            left[rows, :] = dot(active, down)
-            right[rows, :] = dot(grad_pre_b, up, NT)
-
-        @pl.when(chunk > 0)
-        def _():
-            left[rows, :] = left[rows, :] + dot(active, down)
-            right[rows, :] = right[rows, :] + dot(grad_pre_b, up, NT)
-
-        @pl.when(block == 0)
-        def _():
-            grad_proj[units_of, :] = dot(active, grad_in, TN)
-            grad_hidden[:, units_of] = dot(rows_in, grad_pre_b, TN)
-
-        @pl.when(block > 0)
-        def _():
-            grad_proj[units_of, :] = grad_proj[units_of, :] + dot(active, grad_in, TN)
-            grad_hidden[:, units_of] = grad_hidden[:, units_of] + dot(rows_in, grad_pre_b, TN)
+        small[bias_at] = small[bias_at] + bias_grad
+        active, grad_pre_b = jnp.concatenate(actives, axis=0), jnp.concatenate(grads, axis=0)
+        grad_proj[units_of, :] = grad_proj[units_of, :] + dot(active, masked[rows, :], TN)
+        grad_hidden[:, units_of] = grad_hidden[:, units_of] + dot(second[rows, :], grad_pre_b, TN)
 
         @pl.when(chunk == len(chunks) - 1)
         def _():
@@ -703,12 +707,16 @@
 
 
 VMEM_BYTES = 64 * 2**20
-FFN_US, BACK_US, OUTPUT_US, ATTEND_US, FIRST_US, LAST_US = 4.0, 1.4, 1.0, 2.5, 2.0, 2.0
-RATES = (46e3, 1.0, 0.05, 2e6)
+FFN_US, BACK_US, OUTPUT_US, ATTEND_US, FIRST_US, LAST_US = 1.823, 1.279, 0.874, 2.702, 2.067, 2.001
+RATES = (47489.6, 2.462, 0.1, 4e6)
+
+
+KINDS = (0, 1, 2, 0, 1, 3, 0, 1, 2, 0, 1, 3, 0, 1, 2, 0, 1, 3, 0, 1, 2, 0, 1, 3, 0, 1, 2, 0, 1, 3, 0, 1, 2, 0, 1, 3, 0)
+LATER = (0, 0, 0, 0, 0, 2, 0, 0, 0, -1, 0, 0, -2, 0, 0, -2, 0, 0, -1, -2, 0, -2, 0, -2, 3, 8, 5, 7, -6, -7, -9, -4, -4, -6, 2, -2, 2)
 
 
 def urgency(item):
-    return (item[1], item[0])
+    return (item[1] - (-3) * item[2] + LATER[item[1]], item[0])
 
 
 def on_device(
@@ -756,7 +764,7 @@
             shape((hidden, width), f32), shape((width, hidden), f32), shape((128, 128), f32),
             shape((rows, width), f32), shape((rows, width), f32), shape((rows, width), f32),
         ],
-        in_specs=[pl.BlockSpec(memory_space=pltpu.SMEM)] + [anywhere] * 4 + [inside] * 9 + [anywhere] * 4,
+        in_specs=[pl.BlockSpec(memory_space=pltpu.SMEM)] + [anywhere] * 17,
         out_specs=[anywhere] * 12,
         scratch_shapes=[
             pltpu.VMEM((rows, width), f32), pltpu.VMEM((rows, width), f32), pltpu.VMEM((rows, width), f32),
@@ -772,8 +780,9 @@
             pltpu.VMEM((2, PIECE, width), f32), pltpu.VMEM((PIECE, width), bf16),
             pltpu.VMEM((16, hidden), f32), pltpu.VMEM((128, 128), f32),
             *[pltpu.VMEM((width, part), bf16)] * 3, pltpu.VMEM((part, width), bf16),
-            dma((rows // BLOCK + 8,)), dma((2,)), dma, dma((3 * pieces + rows // BLOCK,)), dma((3 * pieces + rows // BLOCK,)),
+            dma((rows // BLOCK + 17,)), dma((2,)), dma, dma((3 * pieces + rows // BLOCK,)), dma((3 * pieces + rows // BLOCK,)),
             dma((units,)), dma((units, stages)), dma((units,)),
+            *[pltpu.VMEM((count,), f32) for count in (width, width, part, part, width, width, width, hidden, width)],
         ],
         compiler_params=pltpu.CompilerParams(
             collective_id=0, has_side_effects=True, vmem_limit_bytes=VMEM_BYTES

time: 268 us -> 264 us (0.985)
  Pallas kernels: 251 us -> 246 us
    pallas_call x1, Pallas kernels: 249 us -> 245 us  [on_device(): pl.pallas_call(functools.partial(layer_kernel, size), out_shape=[shape((r...]
where the time goes in v5:
time: 264 us; the launch traced here: 263 us
  Pallas kernels  246 us (93%)
  local copies, waits for them, and re-layouts  15.3 us (6%)
    pallas_call x1, Pallas kernels, on_device(): pl.pallas_call(functools.partial(layer_kernel, size), out_shape=[shape((r...  245 us
    unnamed x26, local copies, waits for them, and re-layouts  15.3 us

profile of v5, /device:TPU:0, one launch (start us, length us, event | category | flops | bytes accessed | tf_op | source)
XLA Modules:
  0.0 263.0 jit_solution(11446685683764958208)
XLA Ops:
  1.3 244.8 %layer.1 = (bf16[1536,768]{1,0:T(8,128)(2,1)}, bf16[1536,768]{1,0:T(8,128)(2,1)}, f32[768,384]{1,0:T(8,128)}, f32[768,384]{1,0:T(8,128)}, f32[768,384]{1,0:T(8,1...) custom-call(s32[1]{0:T(128)S(6)} %copy.43.length_ref, ...), custom_call_target="tpu_custom_call" | custom-call | tf_op jit(solution)/shard_map/layer/pallas_call | solution.py:759
  246.1 0.0 copy-start
  246.1 1.6 unpack.1
  247.7 0.0 slice-start.2
  247.7 3.4 %copy.44 = bf16[1,1536,768]{2,1,0:T(8,128)(2,1)} copy(bf16[1,1536,768]{2,1,0:T(8,128)(2,1)} %bitcast.9) | data formatting | bytes 4718592
  251.1 0.0 copy-done
  251.1 0.0 copy-start.4
  251.1 0.0 copy-start.3
  251.1 1.4 copy.45
  252.5 0.7 copy-done.4
  253.2 0.0 copy-start.2
  253.2 0.0 slice-start.3
  253.2 1.0 copy.46
  254.2 0.0 copy-done.3
  254.2 0.0 copy-start.1
  254.2 1.0 copy.47
  255.2 0.0 copy-done.2
  255.2 1.0 copy.48
  256.2 0.0 copy-done.1
  256.2 0.0 slice-start
  256.2 1.0 copy.49
  257.2 0.0 slice-done.2
  257.3 0.0 slice-done.3
  257.3 0.0 slice-start.1
  257.3 2.4 copy.50
  259.7 0.8 slice-done
  260.5 0.3 slice-done.1
  260.8 2.2 copy.51
  (2 shorter events, 0.0 us)
Async XLA Ops:
  246.1 5.0 %copy-start = (bf16[1536,768]{1,0:T(8,128)(2,1)S(1)}, bf16[1536,768]{1,0:T(8,128)(2,1)}, u32[]{:S(2)}) copy-start(bf16[1536,768]{1,0:T(8,128)(2,1)} %get-tuple-element.36) | copy-start | bytes 7077892
  247.7 9.5 %slice-start.2 = ((s8[4718592]{0:T(1024)(128)(4,1)}), s8[4194304]{0:T(1024)(128)(4,1)S(1)}, s32[]{:S(2)}) async-start(s8[4718592]{0:T(1024)(128)(4,1)} %bitcast.6), calls=%async_computation.2 | async-start | bytes 8388608
  251.1 2.1 copy-start.4
  251.1 3.1 %copy-start.3 = (f32[768,384]{1,0:T(8,128)S(1)}, f32[768,384]{1,0:T(8,128)}, u32[]{:S(2)}) copy-start(f32[768,384]{1,0:T(8,128)} %get-tuple-element.76) | copy-start | bytes 3538948
  253.2 2.0 copy-start.2
  253.2 4.1 %slice-start.3 = ((s8[4718592]{0:T(1024)(128)(4,1)}), s8[524288]{0:T(1024)(128)(4,1)S(1)}, s32[]{:S(2)}) async-start(s8[4718592]{0:T(1024)(128)(4,1)} %bitcast.6), calls=%async_computation.3 | async-start | bytes 1048576
  254.2 2.0 copy-start.1
  256.2 4.2 %slice-start = ((s8[4718592]{0:T(1024)(128)(4,1)}), s8[4194304]{0:T(1024)(128)(4,1)S(1)}, s32[]{:S(2)}) async-start(s8[4718592]{0:T(1024)(128)(4,1)} %bitcast.4), calls=%async_computation | async-start | bytes 8388608
  257.3 3.5 %slice-start.1 = ((s8[4718592]{0:T(1024)(128)(4,1)}), s8[524288]{0:T(1024)(128)(4,1)S(1)}, s32[]{:S(2)}) async-start(s8[4718592]{0:T(1024)(128)(4,1)} %bitcast.4), calls=%async_computation.1 | async-start | bytes 1048576

commit v6 on v5

--- a/solution.py
+++ b/solution.py
@@ -315,7 +315,7 @@
         Row(ref) for ref in (gain_one, shift_one, query_bias, value_bias, output_bias, gain_two, shift_two, proj_bias)
     )
     (
-        left, right, resid, second, masked, hidden_w, proj_w, queries, keys, values, lse_terms, attended, key_terms,
+        left, right, resid, second, masked, hidden_w, proj_w, queries, keys, values, log_sums, attended, key_terms,
         grad_proj, grad_hidden, *land_hidden, land_attend, land_output, land_small,
         fetched, staged, small, packed, query_weight, key_weight, value_weight, output_weight,
         load_sems, fetch_sem, stage_sem, peer_send, peer_recv, unit_send, unit_recv, unit_own,
@@ -469,6 +469,8 @@
             return dot(jnp.concatenate([query_one, first_term], axis=1), key_all, NT)
 
         mixed = []
+        all_maxima = jnp.zeros((BLOCK, PAIR), jnp.float32)
+        all_totals = jnp.ones((BLOCK, PAIR), jnp.float32)
         upcoming = scores_of(0)
         for number in range(6):
             scores = scores_of(number) if extra and number else upcoming
@@ -480,10 +482,12 @@
             mixture = dot(weights, jnp.concatenate([values[:, cols], ones], axis=1))
             totals = mixture[:, PAIR:]
             mixed.append(mixture[:, :PAIR] / totals)
-            lse_terms[rows, pl.ds(number * PAIR, PAIR)] = minus_in_three(maxima + jnp.log(totals), 1.0)
+            all_maxima = jnp.where(lane == number, maxima, all_maxima)
+            all_totals = jnp.where(lane == number, totals, all_totals)
             if number % 2:
                 attended[rows, cols] = jnp.where(heads[0], mixed[-2], mixed[-1]).astype(jnp.bfloat16)
 
+        log_sums[rows, :] = all_maxima + jnp.log(all_totals)
         right[rows, :] = dot(attended[rows, :], output_weight[...])
         to_peer(right.at[rows, :], left.at[rows, :], step).start()
 
@@ -611,7 +615,8 @@
             query_one = jnp.where(mine, query_pair, jnp.zeros_like(query_pair))
             grad_one = jnp.where(mine, grad_pair, jnp.zeros_like(grad_pair))
             delta = jnp.sum(jnp.where(mine, product, 0.0), axis=1, keepdims=True)
-            terms = lse_terms[part, pl.ds(pl.multiple_of((2 * pair + head) * PAIR, PAIR), PAIR)]
+            log_sum = jnp.sum(jnp.where(lane == 2 * pair + head, log_sums[part, :], 0.0), axis=1, keepdims=True)
+            terms = minus_in_three(log_sum, 1.0)
             probs = jnp.exp(dot(key_all, jnp.concatenate([query_one, terms], axis=1), NT))
             shifted = dot(value_all, jnp.concatenate([grad_one, minus_in_three(delta, 0.0)], axis=1), NT)
             grad_scores = (probs * shifted).astype(jnp.bfloat16)
@@ -707,12 +712,12 @@
 
 
 VMEM_BYTES = 64 * 2**20
-FFN_US, BACK_US, OUTPUT_US, ATTEND_US, FIRST_US, LAST_US = 1.823, 1.279, 0.874, 2.702, 2.067, 2.001
-RATES = (47489.6, 2.462, 0.1, 4e6)
+FFN_US, BACK_US, OUTPUT_US, ATTEND_US, FIRST_US, LAST_US = 1.812, 1.279, 0.871, 2.702, 2.118, 2.117
+RATES = (47496.7, 2.386, 0.1, 4e6)
 
 
 KINDS = (0, 1, 2, 0, 1, 3, 0, 1, 2, 0, 1, 3, 0, 1, 2, 0, 1, 3, 0, 1, 2, 0, 1, 3, 0, 1, 2, 0, 1, 3, 0, 1, 2, 0, 1, 3, 0)
-LATER = (0, 0, 0, 0, 0, 2, 0, 0, 0, -1, 0, 0, -2, 0, 0, -2, 0, 0, -1, -2, 0, -2, 0, -2, 3, 8, 5, 7, -6, -7, -9, -4, -4, -6, 2, -2, 2)
+LATER = (0, -1, 0, 0, -3, 3, 0, 0, 3, -1, 0, 0, -2, 0, 0, -2, 0, 0, 1, 0, 0, -2, 1, 3, 1, 1, 0, 7, -3, -1, -6, 5, -4, -8, 8, -4, 0)
 
 
 def urgency(item):
@@ -771,7 +776,7 @@
             pltpu.VMEM((rows, width), bf16), pltpu.VMEM((rows, width), bf16),
             pltpu.VMEM((width, hidden), bf16), pltpu.VMEM((hidden, width), bf16),
             pltpu.VMEM((rows, part), bf16), pltpu.VMEM((rows, part), bf16), pltpu.VMEM((rows, part), bf16),
-            pltpu.VMEM((rows, 2 * part), bf16), pltpu.VMEM((rows, part), bf16), pltpu.VMEM((rows, PAIR), bf16),
+            pltpu.VMEM((rows, PAIR), f32), pltpu.VMEM((rows, part), bf16), pltpu.VMEM((rows, PAIR), bf16),
             pltpu.VMEM((hidden, width), f32), pltpu.VMEM((width, hidden), f32),
             *chunk_lands,
             pltpu.VMEM((9, landing_rows(256, extra), 384), f32),

time: 264 us -> 263 us (level)
  no operation moved by 1% of the time
where the time goes in v6:
time: 263 us; the launch traced here: 262 us
  Pallas kernels  246 us (94%)
  local copies, waits for them, and re-layouts  15.3 us (6%)
    pallas_call x1, Pallas kernels, on_device(): pl.pallas_call(functools.partial(layer_kernel, size), out_shape=[shape((r...  244 us
    unnamed x26, local copies, waits for them, and re-layouts  15.3 us

profile of v6, /device:TPU:0, one launch (start us, length us, event | category | flops | bytes accessed | tf_op | source)
XLA Modules:
  0.0 262.2 jit_solution(16504054587444785519)
XLA Ops:
  1.3 244.0 %layer.1 = (bf16[1536,768]{1,0:T(8,128)(2,1)}, bf16[1536,768]{1,0:T(8,128)(2,1)}, f32[768,384]{1,0:T(8,128)}, f32[768,384]{1,0:T(8,128)}, f32[768,384]{1,0:T(8,1...) custom-call(s32[1]{0:T(128)S(6)} %copy.43.length_ref, ...), custom_call_target="tpu_custom_call" | custom-call | tf_op jit(solution)/shard_map/layer/pallas_call | solution.py:764
  245.3 0.0 copy-start
  245.3 1.6 unpack.1
  247.0 0.0 slice-start.2
  247.0 3.4 %copy.44 = bf16[1,1536,768]{2,1,0:T(8,128)(2,1)} copy(bf16[1,1536,768]{2,1,0:T(8,128)(2,1)} %bitcast.9) | data formatting | bytes 4718592
  250.3 0.0 copy-done
  250.3 0.0 copy-start.4
  250.3 0.0 copy-start.3
  250.3 1.4 copy.45
  251.7 0.7 copy-done.4
  252.4 0.0 copy-start.2
  252.4 0.0 slice-start.3
  252.4 1.0 copy.46
  253.4 0.0 copy-done.3
  253.5 0.0 copy-start.1
  253.5 1.0 copy.47
  254.5 0.0 copy-done.2
  254.5 1.0 copy.48
  255.5 0.0 copy-done.1
  255.5 0.0 slice-start
  255.5 1.0 copy.49
  256.5 0.0 slice-done.2
  256.5 0.0 slice-done.3
  256.5 0.0 slice-start.1
  256.5 2.4 copy.50
  258.9 0.8 slice-done
  259.7 0.3 slice-done.1
  260.1 2.2 copy.51
  (2 shorter events, 0.0 us)
Async XLA Ops:
  245.3 5.0 %copy-start = (bf16[1536,768]{1,0:T(8,128)(2,1)S(1)}, bf16[1536,768]{1,0:T(8,128)(2,1)}, u32[]{:S(2)}) copy-start(bf16[1536,768]{1,0:T(8,128)(2,1)} %get-tuple-element.36) | copy-start | bytes 7077892
  247.0 9.5 %slice-start.2 = ((s8[4718592]{0:T(1024)(128)(4,1)}), s8[4194304]{0:T(1024)(128)(4,1)S(1)}, s32[]{:S(2)}) async-start(s8[4718592]{0:T(1024)(128)(4,1)} %bitcast.6), calls=%async_computation.2 | async-start | bytes 8388608
  250.3 2.1 copy-start.4
  250.3 3.1 %copy-start.3 = (f32[768,384]{1,0:T(8,128)S(1)}, f32[768,384]{1,0:T(8,128)}, u32[]{:S(2)}) copy-start(f32[768,384]{1,0:T(8,128)} %get-tuple-element.76) | copy-start | bytes 3538948
  252.4 2.0 copy-start.2
  252.4 4.1 %slice-start.3 = ((s8[4718592]{0:T(1024)(128)(4,1)}), s8[524288]{0:T(1024)(128)(4,1)S(1)}, s32[]{:S(2)}) async-start(s8[4718592]{0:T(1024)(128)(4,1)} %bitcast.6), calls=%async_computation.3 | async-start | bytes 1048576
  253.5 2.0 copy-start.1
  255.5 4.2 %slice-start = ((s8[4718592]{0:T(1024)(128)(4,1)}), s8[4194304]{0:T(1024)(128)(4,1)S(1)}, s32[]{:S(2)}) async-start(s8[4718592]{0:T(1024)(128)(4,1)} %bitcast.4), calls=%async_computation | async-start | bytes 8388608
  256.5 3.5 %slice-start.1 = ((s8[4718592]{0:T(1024)(128)(4,1)}), s8[524288]{0:T(1024)(128)(4,1)S(1)}, s32[]{:S(2)}) async-start(s8[4718592]{0:T(1024)(128)(4,1)} %bitcast.4), calls=%async_computation.1 | async-start | bytes 1048576
